TPU v7x, 256 devices: a whole 4x4x8 slice. The times are simulated.
256 devices in a mesh: roll: 4 (over z_lo), seq: 16 (over y, x), tp: 4 (over z_hi, core).
Axes of the slice: x: 4, y: 4, z: 8 (z_hi: 2, z_lo: 4; z = z_hi * 4 + z_lo), core: 2. Of those that a mesh axis runs over, the one named last changes fastest.
Arguments:
- prompt_kv: bfloat16 [2, 256, 1024], P(None, ('roll', 'seq', 'tp')), may hold values from -6 to 6
- comp_q: bfloat16 [4, 2048, 8192], P('roll', 'seq', 'tp'), may hold values from -6 to 6
- comp_kv: bfloat16 [2, 4, 2048, 1024], P(None, 'roll', 'seq', 'tp'), may hold values from -6 to 6
- out_grad: bfloat16 [4, 2048, 8192], P('roll', 'seq', 'tp'), may hold values from -6 to 6
- lengths: int32 [4], P('roll'), may hold values from 256 to 2048, as said below
Outputs:
- attn_out: bfloat16 [4, 2048, 8192], P('roll', 'seq', 'tp')
- q_grad: bfloat16 [4, 2048, 8192], P('roll', 'seq', 'tp')
- comp_kv_grad: float32 [2, 4, 2048, 1024], P(None, 'roll', 'seq', 'tp')
- prompt_kv_grad: float32 [2, 256, 1024], P(None, ('roll', 'seq'), 'tp')
Inputs may be any that keep to these rules, and one draw needn't show every extreme that they name: `lengths`: positions at or beyond a rollout's length are padding. In every draw one rollout uses all 2048 positions and one an eighth of them.
All inputs are finite; a program needn't handle non-finite values.
Results may differ from a plain program's by a relative error of at most 0.0088.
Values may be sent and summed in bfloat16 or wider, within the bound.
A program may use at most 64 MiB of HBM per device.

v0:
```python
import math

import jax
import jax.numpy as jnp
from jax import lax
from jax.sharding import PartitionSpec as P

HD = 128


floor_score = -1e30


def split_heads(matrix, kv_count):
    row_count = matrix.shape[0]
    grouped = matrix.reshape(row_count, kv_count, -1, HD)
    return grouped.transpose(1, 2, 0, 3)


def join_heads(tensor):
    kv_count, group_size, row_count, head_width = tensor.shape
    return tensor.transpose(2, 0, 1, 3).reshape(row_count, kv_count * group_size * head_width)


def key_slab(key_rows, first_key, slab_rows, kv_count):
    slab = lax.dynamic_slice_in_dim(key_rows, first_key, slab_rows, 0)
    return slab.reshape(slab_rows, kv_count, HD)


def block_scores(query_heads, key_part, score_scale):
    return (
        jnp.einsum("kgrd,nkd->kgrn", query_heads, key_part, preferred_element_type=jnp.float32)
        * score_scale
    )


def attend_half(
    query_part, grad_part, query_start, length, prompt_keys, own_keys, prompt_grads, own_grads
):
    kv_count = prompt_keys.shape[2] // HD
    score_scale = 1.0 / math.sqrt(HD)
    half_rows = query_part.shape[0]
    query_heads = split_heads(query_part, kv_count)
    query_pos = query_start + jnp.arange(half_rows, dtype=jnp.int32)
    query_live = query_pos < length
    grad_masked = jnp.where(query_live[:, None], grad_part, jnp.zeros_like(grad_part))
    grad_heads = split_heads(grad_masked, kv_count)
    prompt_span = min(256, prompt_keys.shape[1])
    prompt_blocks = prompt_keys.shape[1] // prompt_span
    own_span = min(256, own_keys.shape[1])
    reach_end = jnp.minimum(query_start + half_rows, length)
    own_blocks = jnp.where(query_start < length, (reach_end + own_span - 1) // own_span, 0)

    def prompt_scores(block_index):
        first_key = block_index * prompt_span
        key_part = key_slab(prompt_keys[0], first_key, prompt_span, kv_count)
        return (block_scores(query_heads, key_part, score_scale), first_key)

    def own_scores(block_index):
        first_key = block_index * own_span
        key_part = key_slab(own_keys[0], first_key, own_span, kv_count)
        scores = block_scores(query_heads, key_part, score_scale)
        key_pos = first_key + jnp.arange(own_span, dtype=jnp.int32)
        allowed = (key_pos[None, :] <= query_pos[:, None]) & (key_pos[None, :] < length)
        return (jnp.where(allowed[None, None], scores, floor_score), first_key)

    def stats_step(scores_fn):

        def stats_advance(block_index, carried):
            running_max, running_sum = carried
            scores, first_key = scores_fn(block_index)
            new_max = jnp.maximum(running_max, jnp.max(scores, axis=-1))
            running_sum = running_sum * jnp.exp(running_max - new_max) + jnp.sum(
                jnp.exp(scores - new_max[..., None]), axis=-1
            )
            return (new_max, running_sum)

        return stats_advance

    start_max = jnp.full(query_heads.shape[:3], floor_score, jnp.float32)
    statistics = (start_max, jnp.zeros(query_heads.shape[:3], jnp.float32))
    statistics = lax.fori_loop(0, prompt_blocks, stats_step(prompt_scores), statistics)
    statistics = lax.fori_loop(0, own_blocks, stats_step(own_scores), statistics)
    row_max, row_sum = statistics

    def weights_of(scores):
        return jnp.exp(scores - row_max[..., None]) / row_sum[..., None]

    def output_step(scores_fn, value_rows):

        def output_advance(block_index, weighted):
            scores, first_key = scores_fn(block_index)
            slab_rows = scores.shape[-1]
            rounded = weights_of(scores).astype(jnp.bfloat16)
            value_part = key_slab(value_rows, first_key, slab_rows, kv_count)
            return weighted + jnp.einsum(
                "kgrn,nkd->kgrd", rounded, value_part, preferred_element_type=jnp.float32
            )

        return output_advance

    weighted = jnp.zeros(query_heads.shape, jnp.float32)
    weighted = lax.fori_loop(0, prompt_blocks, output_step(prompt_scores, prompt_keys[1]), weighted)
    weighted = lax.fori_loop(0, own_blocks, output_step(own_scores, own_keys[1]), weighted)
    mixed = join_heads(weighted)
    output = jnp.where(query_live[:, None], mixed, 0.0).astype(jnp.bfloat16)
    row_delta = jnp.sum(grad_heads.astype(jnp.float32) * weighted, axis=-1)

    def grad_step(scores_fn, key_rows, value_rows):

        def grad_advance(block_index, carried):
            query_grad, key_grads = carried
            scores, first_key = scores_fn(block_index)
            slab_rows = scores.shape[-1]
            weights = weights_of(scores)
            key_part = key_slab(key_rows, first_key, slab_rows, kv_count)
            value_part = key_slab(value_rows, first_key, slab_rows, kv_count)
            weight_grad = jnp.einsum(
                "kgrd,nkd->kgrn", grad_heads, value_part, preferred_element_type=jnp.float32
            )
            score_grad = (score_scale * weights * (weight_grad - row_delta[..., None])).astype(
                jnp.bfloat16
            )
            query_grad = query_grad + jnp.einsum(
                "kgrn,nkd->kgrd", score_grad, key_part, preferred_element_type=jnp.float32
            )
            key_term = jnp.einsum(
                "kgrn,kgrd->nkd", score_grad, query_heads, preferred_element_type=jnp.float32
            )
            value_term = jnp.einsum(
                "kgrn,kgrd->nkd",
                weights.astype(jnp.bfloat16),
                grad_heads,
                preferred_element_type=jnp.float32,
            )
            fresh = jnp.stack([key_term.reshape(slab_rows, -1), value_term.reshape(slab_rows, -1)])
            previous = lax.dynamic_slice_in_dim(key_grads, first_key, slab_rows, 1)
            key_grads = lax.dynamic_update_slice_in_dim(key_grads, previous + fresh, first_key, 1)
            return (query_grad, key_grads)

        return grad_advance

    query_grad = jnp.zeros(query_heads.shape, jnp.float32)
    query_grad, prompt_grads = lax.fori_loop(
        0,
        prompt_blocks,
        grad_step(prompt_scores, prompt_keys[0], prompt_keys[1]),
        (query_grad, prompt_grads),
    )
    query_grad, own_grads = lax.fori_loop(
        0, own_blocks, grad_step(own_scores, own_keys[0], own_keys[1]), (query_grad, own_grads)
    )
    return (output, join_heads(query_grad).astype(jnp.bfloat16), prompt_grads, own_grads)


def shards(prompt_kv, comp_q, comp_kv, out_grad, lengths):
    seq_index = lax.axis_index("seq")
    shard_rows = comp_q.shape[1]
    half_rows = shard_rows // 2
    heads_piece = lax.all_to_all(prompt_kv, "tp", split_axis=2, concat_axis=1, tiled=True)
    prompt_keys = lax.all_gather(heads_piece, ("roll", "seq"), axis=1, tiled=True)
    own_keys = lax.all_gather(comp_kv, "seq", axis=2, tiled=True)
    prompt_grads = jnp.zeros(prompt_keys.shape, jnp.float32)
    length = lengths[0]
    keys_here = own_keys[:, 0]
    grads_here = jnp.zeros(keys_here.shape, jnp.float32)
    lower_start = seq_index * shard_rows
    lower_out, lower_grad, prompt_grads, grads_here = attend_half(
        comp_q[0, :half_rows],
        out_grad[0, :half_rows],
        lower_start,
        length,
        prompt_keys,
        keys_here,
        prompt_grads,
        grads_here,
    )
    upper_query = comp_q[0, half_rows:]
    upper_cotangent = out_grad[0, half_rows:]
    upper_start = lower_start + half_rows
    upper_out, upper_grad, prompt_grads, grads_here = attend_half(
        upper_query,
        upper_cotangent,
        upper_start,
        length,
        prompt_keys,
        keys_here,
        prompt_grads,
        grads_here,
    )
    out_parts = [jnp.concatenate([lower_out, upper_out], axis=0)]
    grad_parts = [jnp.concatenate([lower_grad, upper_grad], axis=0)]
    own_parts = [grads_here]
    own_grads = jnp.stack(own_parts, axis=1)
    own_sum = lax.psum_scatter(own_grads, "seq", scatter_dimension=2, tiled=True)
    prompt_sum = lax.psum_scatter(prompt_grads, ("roll", "seq"), scatter_dimension=1, tiled=True)
    return (jnp.stack(out_parts), jnp.stack(grad_parts), own_sum, prompt_sum)


def solution(mesh):
    in_specs = (
        P(None, ("roll", "seq", "tp"), None),
        P("roll", "seq", "tp"),
        P(None, "roll", "seq", "tp"),
        P("roll", "seq", "tp"),
        P("roll"),
    )
    out_specs = (
        P("roll", "seq", "tp"),
        P("roll", "seq", "tp"),
        P(None, "roll", "seq", "tp"),
        P(None, ("roll", "seq"), "tp"),
    )
    return jax.shard_map(shards, mesh=mesh, in_specs=in_specs, out_specs=out_specs, check_vma=False)
```

profile of v0, /device:TPU:4, one launch (start us, length us, event | category | flops | bytes accessed | tf_op | source)
XLA Modules:
  0.0 1184.1 jit_solution(16545110488446760774)
XLA Ops:
  7.2 1.7 copy.160
  8.9 1.1 copy.155
  10.5 2.3 reduce
  12.8 0.9 reshape.528
  13.7 8.5 all-to-all-start
  22.8 1.1 slice_bitcast_fusion.5
  23.9 1.1 slice_bitcast_fusion.3
  25.0 0.6 add_compare_fusion
  25.8 0.8 copy.265
  26.6 0.7 copy.267
  27.3 2.5 all-to-all-done
  29.9 0.6 reshape.529
  30.8 179.8 %all_gather.6 = bf16[2,256,256]{2,0,1:T(2,128)(2,1)S(1)} all-gather(bf16[2,4,256]{2,0,1:T(2,128)(2,1)S(1)} %bitcast.475), channel_id=1, replica_groups=mesh['roll'=4,'seq'=16,'tp'=4] {'roll','seq'}, dimensions={1}, use_global_device_ids=true | all-gather | bytes 266240 | tf_op jit(solution)/shard_map/all_gather | solution.py:161
  211.6 1.0 copy-done.8
  213.4 1.0 copy-done.7
  214.8 0.6 multiply_add_fusion.2
  215.4 0.6 multiply_add_fusion.3
  216.0 1.7 fusion.77
  217.7 1.1 fusion.90
  218.8 1.5 slice_bitcast_fusion
  220.3 2.3 fusion.74
  222.6 1.2 fusion.70
  223.9 0.9 copy.179
  224.8 1.9 fusion.67
  226.7 1.0 fusion.81
  227.7 1.1 fusion.92
  229.4 1.6 fusion.76
  231.0 1.1 fusion.89
  232.1 2.3 fusion.75
  234.4 1.2 fusion.72
  235.7 1.5 copy.171
  237.2 1.9 fusion.66
  239.1 1.0 fusion.80
  240.1 1.1 fusion.91
  241.2 1.1 copy.189
  242.3 1.8 copy.190
  244.1 1.8 copy.186
  245.9 1.8 copy.187
  247.7 2.0 maximum_add_fusion.2
  249.8 2.5 broadcast_in_dim.155
  252.3 0.7 copy-done.24
  252.9 5.4 copy.184
  258.4 0.6 copy-done.28
  261.8 0.8 maximum_bitcast_fusion
  262.7 0.8 maximum_bitcast_fusion.1
  263.5 828.0 %all-reduce.3.cloned.1.call-done = f32[2,256,256]{2,1,0:T(8,128)} async-done(((f32[2,256,256]{2,1,0:T(8,128)}), f32[2,256,256]{2,1,0:T(8,128)}) %all-reduce.3.cloned.1.call-update) | async-done | bytes 524304
  1091.5 1.3 constant_dynamic-slice_fusion.12
  1092.9 84.8 %reduce-scatter.3.cloned.1.call-done = f32[2,1,128,256]{3,2,1,0:T(8,128)} async-done(((f32[2,1,2048,256]{3,2,1,0:T(8,128)}), f32[2,1,128,256]{3,2,1,0:T(8,128)}) %reduce-scatter.3.cloned.1.call-update) | async-done | bytes 262160 | tf_op jit(solution)/shard_map/reduce_scatter | solution.py:195
  (87 shorter events, 6.2 us)
Async XLA Ops:
  7.2 208.8 %all-gather.2.cloned.1.call-start = ((), (), s32[]{:S(2)}) async-start(), calls=%async_computation.2 | async-start | bytes 2228224 | tf_op jit(solution)/shard_map/all_gather | solution.py:162
  13.7 16.2 %all-to-all-start = ((bf16[4,2,256]{2,1,0:T(2,128)(2,1)}), bf16[4,2,256]{2,1,0:T(2,128)(2,1)S(1)}, u32[]{:S(2)}, u32[]{:S(2)}) async-start(bf16[4,2,256]{2,1,0:T(2,128)(2,1)} %reshape.528), calls=%async_computation | async-start | bytes 8192 | tf_op jit(solution)/shard_map/all_to_all | solution.py:160
  22.2 1069.4 %all-reduce.3.cloned.1.call-start = ((), (), s32[]{:S(2)}) async-start(), calls=%async_computation.4 | async-start | bytes 1048576
  25.6 187.8 %copy-start.11 = (bf16[8,8,16,128]{3,2,1,0:T(8,128)(2,1)}, bf16[8,8,16,128]{3,2,1,0:T(8,128)(2,1)S(1)}, u32[]{:S(2)}) copy-start(bf16[8,8,16,128]{3,2,1,0:T(8,128)(2,1)S(1)} %copy.261) | copy-start | bytes 786436
  211.1 6.7 copy-start.18
  211.2 4.8 copy-start.13
  211.6 1.0 copy-start.8
  213.4 1.0 copy-start.7
  216.0 2.8 copy-start
  222.6 1.2 copy-start.17
  222.6 5.0 copy-start.14
  223.8 5.0 copy-start.20
  224.8 4.0 copy-start.23
  228.8 2.2 copy-start.19
  228.8 0.6 copy-start.21
  234.4 1.2 copy-start.16
  234.4 5.7 copy-start.15
  235.6 3.5 copy-start.12
  241.2 11.0 copy-start.22
  241.2 11.0 copy-start.25
  249.7 927.9 %reduce-scatter.3.cloned.1.call-start = ((), (), s32[]{:S(2)}) async-start(), calls=%async_computation.3 | async-start | bytes 4456448 | tf_op jit(solution)/shard_map/reduce_scatter | solution.py:195
  252.2 0.7 copy-start.24
  258.4 0.7 copy-start.28
  258.4 1.9 copy-start.9
  258.4 2.2 copy-start.10
  258.4 2.6 copy-start.3
  258.4 2.9 copy-start.6
  258.4 3.2 copy-start.27
  258.4 3.3 copy-start.26
Sparse Core Ops, SparseCore 0:
  11.0 54.1 all-gather.1
  249.9 841.6 all-reduce.2
  1096.2 81.3 reduce-scatter.2
where the time goes:
time: 1190 us; the launch traced here: 1180 us
  waiting for transfers between devices  915 us (77%)
  blocking collectives  180 us (15%)
  local copies, waits for them, and re-layouts  35 us (3%)
  other arithmetic  16.8 us (1%)
  between operations  15.5 us (1%)
  matrix products  13.2 us (1%)
    unnamed x4, waiting for transfers between devices  828 us
    all_gather x1, blocking collectives, shards(): lax.all_gather(heads_piece, ('roll', 'seq'), axis=1, tiled=True)  180 us
    reduce_scatter x1, waiting for transfers between devices, shards(): lax.psum_scatter(own_grads, 'seq', scatter_dimension=2, tiled=True)  84.8 us
  transfers between devices with their start and end apart: 4, of which 3 were waited for; matrix products, arithmetic and copies ran while one was open for 2% of the time, Pallas kernels for 0%

commit v1 on v0

v1 whole, which is shorter than its diff:
```python
import math

import jax
import jax.numpy as jnp
from jax import lax
from jax.experimental import pallas as pl
from jax.experimental.pallas import tpu as pltpu
from jax.sharding import PartitionSpec as P

HD = 128
BLOCK = 128
GROUP = 8
ROWS = GROUP * BLOCK
SLAB = 4 * BLOCK
PROMPT = 256
SCALE = 1.0 / math.sqrt(HD)
LOG2_SCALE = SCALE * math.log2(math.e)
FLOOR = -1e30
f32 = jnp.float32
bf16 = jnp.bfloat16
MESH = pl.DeviceIdType.MESH


def dot_nt(a, b):
    return lax.dot_general(a, b, (((1,), (1,)), ((), ())), preferred_element_type=f32)


def dot_nn(a, b):
    return lax.dot_general(a, b, (((1,), (0,)), ((), ())), preferred_element_type=f32)


def eye(n):
    rows = lax.broadcasted_iota(jnp.int32, (n, n), 0)
    cols = lax.broadcasted_iota(jnp.int32, (n, n), 1)
    return jnp.where(rows == cols, 1.0, 0.0).astype(bf16)


def rem4(i):
    return lax.rem(i, 4)


def rem16(i):
    return lax.rem(i, 16)


def kernel(
    len_ref, pk_ref, q_ref, kv_ref, do_ref,
    out_ref, qg_ref, okv_ref, opk_ref,
    qs, dos, kvb, pb, pp, mc, mx, sm, o_t, dq_t, dl, acc,
    ds_part, own, m1, m2, tot, tsend, n1, n2,
    buf_a, buf_a2, buf_b, pgs, rec_c, src_d, rec_d,
    s1, r1, s2, r2, sm1, rm1, sm2, rm2, sn1, rn1, sn2, rn2,
    s_a, r_a, s_b, r_b, s_c, r_c, s_d, r_d,
):
    roll = lax.axis_index("roll")
    seq = lax.axis_index("seq")
    tp = lax.axis_index("tp")
    y = lax.div(seq, 4)
    x = rem4(seq)
    col = roll * 4 + tp
    length = len_ref[0]

    def x_dev(d):
        return {"seq": y * 4 + rem4(x + d)}

    def y_dev(d):
        return {"seq": rem4(y + d) * 4 + x}

    def seq_dev(d):
        return {"seq": rem16(seq + d)}

    def col_dev(d):
        c = rem16(col + d)
        return {"roll": lax.div(c, 4), "tp": rem4(c)}

    def inner(g, d):
        return x_dev(d) if g == 0 else y_dev(d)

    def outer(g, d):
        return y_dev(d) if g == 0 else x_dev(d)

    def slab_of(g):
        return y if g == 0 else x

    def block_of(g):
        return x if g == 0 else y

    def rcopy(src, dst, ssem, rsem, dev):
        return pltpu.make_async_remote_copy(
            src_ref=src, dst_ref=dst, send_sem=ssem, recv_sem=rsem, device_id=dev, device_id_type=MESH
        )

    def rows_of(b):
        return pl.ds(pl.multiple_of(b * BLOCK, BLOCK), BLOCK)

    barrier = pltpu.get_barrier_semaphore()

    @pl.loop(1, 16)
    def _(d):
        pl.semaphore_signal(barrier, inc=1, device_id=seq_dev(d), device_id_type=MESH)
        pl.semaphore_signal(barrier, inc=1, device_id=col_dev(d), device_id_type=MESH)

    for g in range(2):
        for kv in range(2):
            kvb[g, slab_of(g), kv, rows_of(block_of(g)), :] = kv_ref[kv, :, g * HD : (g + 1) * HD]
    buf_a[pl.ds(pl.multiple_of(col * 8, 8), 8), :] = pk_ref[tp]

    pl.semaphore_wait(barrier, 30)

    def block_send(g, k):
        o, b = slab_of(g), block_of(g)
        if k == 0:
            ref, d = kvb.at[g, o, :, rows_of(b), :], 1
        elif k == 1:
            ref, d = kvb.at[g, o, :, rows_of(b), :], 3
        elif k == 2:
            ref, d = kvb.at[g, o, 0, rows_of(rem4(b + 3)), :], 1
        else:
            ref, d = kvb.at[g, o, 1, rows_of(rem4(b + 1)), :], 3
        return rcopy(ref, ref, s1.at[g, k], r1.at[g, k], inner(g, d))

    def block_recv(g, k):
        o, b = slab_of(g), block_of(g)
        if k == 0:
            ref = kvb.at[g, o, :, rows_of(rem4(b + 3)), :]
        elif k == 1:
            ref = kvb.at[g, o, :, rows_of(rem4(b + 1)), :]
        elif k == 2:
            ref = kvb.at[g, o, 0, rows_of(rem4(b + 2)), :]
        else:
            ref = kvb.at[g, o, 1, rows_of(rem4(b + 2)), :]
        return rcopy(ref, ref, s1.at[g, k], r1.at[g, k], inner(g, 1))

    def slab_send(g, k):
        o = slab_of(g)
        if k == 0:
            ref, d = kvb.at[g, o], 1
        elif k == 1:
            ref, d = kvb.at[g, o], 3
        elif k == 2:
            ref, d = kvb.at[g, rem4(o + 3), 0], 1
        else:
            ref, d = kvb.at[g, rem4(o + 1), 1], 3
        return rcopy(ref, ref, s2.at[g, k], r2.at[g, k], outer(g, d))

    def slab_recv(g, k):
        o = slab_of(g)
        if k == 0:
            ref = kvb.at[g, rem4(o + 3)]
        elif k == 1:
            ref = kvb.at[g, rem4(o + 1)]
        else:
            ref = kvb.at[g, rem4(o + 2), k - 2]
        return rcopy(ref, ref, s2.at[g, k], r2.at[g, k], outer(g, 1))

    def a_send(d):
        dev = col_dev(d)
        dst = buf_a.at[pl.ds(pl.multiple_of(col * 8, 8), 8), :]
        return rcopy(pk_ref.at[dev["tp"]], dst, s_a.at[d], r_a.at[d], dev)

    def a_recv(d):
        c = rem16(col + 16 - d)
        ref = buf_a.at[pl.ds(pl.multiple_of(c * 8, 8), 8), :]
        return rcopy(pk_ref.at[tp], ref, s_a.at[d], r_a.at[d], col_dev(d))

    def seq_rows(s):
        return pl.ds(pl.multiple_of(s * 16, 16), 16)

    def b_send(d):
        return rcopy(buf_a2, buf_b.at[:, seq_rows(seq), :], s_b.at[d], r_b.at[d], seq_dev(d))

    def b_recv(d):
        s = rem16(seq + 16 - d)
        return rcopy(buf_a2, buf_b.at[:, seq_rows(s), :], s_b.at[d], r_b.at[d], seq_dev(d))

    def c_send(d):
        s = rem16(seq + d)
        return rcopy(pgs.at[:, seq_rows(s), :], rec_c.at[seq], s_c.at[d], r_c.at[d], seq_dev(d))

    def c_recv(d):
        s = rem16(seq + 16 - d)
        return rcopy(rec_c.at[s], rec_c.at[s], s_c.at[d], r_c.at[d], seq_dev(d))

    def d_send(d):
        r = rem4(roll + d)
        return rcopy(src_d.at[r], rec_d.at[roll], s_d.at[d], r_d.at[d], {"roll": r})

    def d_recv(d):
        r = rem4(roll + 4 - d)
        return rcopy(rec_d.at[r], rec_d.at[r], s_d.at[d], r_d.at[d], {"roll": r})

    for k in range(2):
        for g in range(2):
            block_send(g, k).start()

    @pl.loop(1, 16)
    def _(d):
        a_send(d).start()

    live_rows = seq * BLOCK + lax.broadcasted_iota(jnp.int32, (BLOCK, HD), 0) < length
    for g in range(2):
        for h in range(GROUP):
            cols = slice((g * GROUP + h) * HD, (g * GROUP + h + 1) * HD)
            rows = slice(h * BLOCK, (h + 1) * BLOCK)
            qs[g, rows, :] = q_ref[:, cols]
            dos[g, rows, :] = jnp.where(live_rows, do_ref[:, cols].astype(f32), 0.0).astype(bf16)
    mx[...] = jnp.full(mx.shape, FLOOR, f32)
    sm[...] = jnp.zeros(sm.shape, f32)
    o_t[...] = jnp.zeros(o_t.shape, f32)
    dq_t[...] = jnp.zeros(dq_t.shape, f32)

    for g in range(2):
        block_recv(g, 0).wait_recv()
        block_send(g, 2).start()
        block_recv(g, 1).wait_recv()
        block_send(g, 3).start()

    @pl.loop(1, 16)
    def _(d):
        a_recv(d).wait_recv()

    for j in range(4):
        buf_a2[j] = buf_a[pl.ds(j, 16, stride=8), :].astype(bf16)

    @pl.loop(1, 16)
    def _(d):
        b_send(d).start()

    buf_b[:, seq_rows(seq), :] = buf_a2[...]

    for g in range(2):
        block_recv(g, 2).wait_recv()
        block_recv(g, 3).wait_recv()
        slab_send(g, 0).start()
        slab_send(g, 1).start()

    def fwd(g, c, k, v, p_ref, mask):
        n = k.shape[0]
        v_t = dot_nt(eye(HD), v).astype(bf16)
        s = dot_nt(k, qs[g]) * LOG2_SCALE
        if mask is not None:
            s = jnp.where(mask(n), s, FLOOR)
        m_old = mx[g]
        m_new = jnp.maximum(m_old, jnp.max(s, axis=0, keepdims=True))
        p = jnp.exp2(s - m_new)
        alpha = jnp.exp2(m_old - m_new)
        mx[g] = m_new
        mc[g, c] = m_new
        sm[g] = sm[g] * alpha + jnp.sum(p, axis=0, keepdims=True)
        rounded = p.astype(bf16)
        p_ref[...] = rounded
        o_t[g] = o_t[g] * alpha + dot_nn(v_t, rounded)

    def pick(g):
        return jnp.where(g == 0, y, x)

    def offset(kind):
        return jnp.where(kind == 2, 1, jnp.where(kind == 3, 3, jnp.where(kind == 4, 2, 0)))

    def fwd_slab(g, slab):
        all_seen = jnp.where(g == 0, slab < y, (y == 3) & (slab < x))
        none_seen = (g == 0) & (slab > y)

        def mask(n):
            row = lax.broadcasted_iota(jnp.int32, (n, 1), 0)
            block = lax.div(row, BLOCK)
            key_block = jnp.where(g == 0, slab * 4 + block, block * 4 + slab)
            key_pos = key_block * BLOCK + lax.rem(row, BLOCK)
            lane = lax.broadcasted_iota(jnp.int32, (1, ROWS), 1)
            return key_pos <= seq * BLOCK + lax.rem(lane, BLOCK)

        @pl.when(all_seen)
        def _():
            fwd(g, slab, kvb[g, slab, 0], kvb[g, slab, 1], pb.at[g, slab], None)

        @pl.when(jnp.logical_not(all_seen | none_seen))
        def _():
            fwd(g, slab, kvb[g, slab, 0], kvb[g, slab, 1], pb.at[g, slab], mask)

    @pl.loop(0, 10)
    def _(i):
        g = lax.rem(i, 2)
        kind = lax.div(i, 2)

        @pl.when(i == 2)
        def _():
            @pl.loop(1, 16)
            def _(d):
                b_recv(d).wait_recv()

        @pl.when(i == 4)
        def _():
            for h in range(2):
                slab_recv(h, 0).wait_recv()
                slab_send(h, 2).start()
                slab_recv(h, 1).wait_recv()
                slab_send(h, 3).start()

        @pl.when(i == 8)
        def _():
            for h in range(2):
                slab_recv(h, 2).wait_recv()
                slab_recv(h, 3).wait_recv()

        @pl.when(kind == 1)
        def _():
            fwd(g, 4, buf_b[g], buf_b[2 + g], pp.at[g], None)

        @pl.when(kind != 1)
        def _():
            fwd_slab(g, rem4(pick(g) + offset(kind)))

    @pl.loop(0, 2)
    def _(g):
        inv = 1.0 / sm[g]
        mixed = o_t[g] * inv
        dl[g] = jnp.sum(dot_nt(eye(HD), dos[g]) * mixed, axis=0, keepdims=True)
        sm[g] = inv
        lane = lax.broadcasted_iota(jnp.int32, (1, ROWS), 1)
        live = seq * BLOCK + lax.rem(lane, BLOCK) < length
        rounded = jnp.where(live, mixed, 0.0).astype(bf16)
        for h in range(GROUP):
            head = dot_nt(eye(BLOCK), rounded[:, h * BLOCK : (h + 1) * BLOCK])
            out_ref[:, pl.ds(pl.multiple_of((g * GROUP + h) * HD, HD), HD)] = head.astype(bf16)

    def bwd(g, c, k, v, p):
        n = k.shape[0]
        k_t = dot_nt(eye(HD), k).astype(bf16)
        factor = jnp.exp2(mc[g, c] - mx[g]) * sm[g]
        dp = dot_nt(v, dos[g])
        w = p.astype(f32) * factor
        ds = (w * (dp - dl[g])).astype(bf16)
        acc[1, :n] = dot_nn(w.astype(bf16), dos[g])
        acc[0, :n] = dot_nn(ds, qs[g]) * SCALE
        dq_t[g] += dot_nn(k_t, ds)

    def order(kind):
        return jnp.where(kind == 0, 2, jnp.where(kind == 1, 1, jnp.where(kind == 2, 3, 0)))

    def m1_send(g, kv):
        return rcopy(ds_part.at[g, 0, kv], m1.at[g, kv], sm1.at[g, kv], rm1.at[g, kv], outer(g, 1 if kv == 0 else 3))

    def m2_send(g, k):
        return rcopy(ds_part.at[g, 1 + k], m2.at[g, k], sm2.at[g, k], rm2.at[g, k], outer(g, 1 if k == 0 else 3))

    @pl.loop(0, 10)
    def _(i):
        g = lax.rem(i, 2)
        kind = lax.div(i, 2)
        slab = rem4(pick(g) + order(kind))
        none_seen = (g == 0) & (slab > y)

        @pl.when(kind == 3)
        def _():
            bwd(g, 4, buf_b[g], buf_b[2 + g], pp[g])
            pgs[g] = acc[0, :PROMPT].astype(bf16)
            pgs[2 + g] = acc[1, :PROMPT].astype(bf16)

        @pl.when((kind != 3) & jnp.logical_not(none_seen))
        def _():
            bwd(g, slab, kvb[g, slab, 0], kvb[g, slab, 1], pb[g, slab])

        @pl.when(none_seen & (kind != 3))
        def _():
            acc[...] = jnp.zeros(acc.shape, f32)

        @pl.when(kind < 3)
        def _():
            ds_part[g, kind] = acc[...].astype(bf16)

        @pl.when(kind == 4)
        def _():
            own[g] = acc[...]

        for h in range(2):

            @pl.when(i == h)
            def _():
                m1_send(h, 0).start()
                m1_send(h, 1).start()

            @pl.when(i == 2 + h)
            def _():
                m1_send(h, 0).wait_recv()
                ds_part[h, 1, 0] = (acc[0] + m1[h, 0].astype(f32)).astype(bf16)
                m2_send(h, 0).start()

            @pl.when(i == 4 + h)
            def _():
                m1_send(h, 1).wait_recv()
                ds_part[h, 2, 1] = (acc[1] + m1[h, 1].astype(f32)).astype(bf16)
                m2_send(h, 1).start()

        @pl.when(i == 7)
        def _():
            rec_c[seq] = pgs[:, seq_rows(seq), :]

            @pl.loop(1, 16)
            def _(d):
                c_send(d).start()

    @pl.loop(0, 2)
    def _(g):
        rounded = (dq_t[g] * SCALE).astype(bf16)
        for h in range(GROUP):
            head = dot_nt(eye(BLOCK), rounded[:, h * BLOCK : (h + 1) * BLOCK])
            qg_ref[:, pl.ds(pl.multiple_of((g * GROUP + h) * HD, HD), HD)] = head.astype(bf16)

    def n1_send(g, kv):
        return rcopy(tsend.at[g, 0, kv], n1.at[g, kv], sn1.at[g, kv], rn1.at[g, kv], inner(g, 1 if kv == 0 else 3))

    def n2_send(g, k):
        return rcopy(tsend.at[g, 1 + k], n2.at[g, k], sn2.at[g, k], rn2.at[g, k], inner(g, 1 if k == 0 else 3))

    for g in range(2):
        b = block_of(g)
        m2_send(g, 0).wait_recv()
        m2_send(g, 1).wait_recv()
        tot[g] = own[g] + m2[g, 0].astype(f32) + m2[g, 1].astype(f32)
        tsend[g, 0] = tot[g, :, rows_of(rem4(b + 2)), :].astype(bf16)
        n1_send(g, 0).start()
        n1_send(g, 1).start()

    @pl.loop(1, 16)
    def _(d):
        c_recv(d).wait_recv()

    total_c = rec_c[0].astype(f32)
    for s in range(1, 16):
        total_c = total_c + rec_c[s].astype(f32)
    for r in range(4):
        part = total_c[:, r * 4 : (r + 1) * 4, :]
        src_d[r] = jnp.concatenate([part, jnp.zeros_like(part)], axis=1)
    for d in range(1, 4):
        d_send(d).start()
    rec_d[roll] = src_d[roll]

    for g in range(2):
        b = block_of(g)
        n1_send(g, 0).wait_recv()
        n1_send(g, 1).wait_recv()
        right = rows_of(rem4(b + 1))
        left = rows_of(rem4(b + 3))
        tsend[g, 1, 0] = (tot[g, 0, right, :] + n1[g, 0].astype(f32)).astype(bf16)
        tsend[g, 1, 1] = tot[g, 1, right, :].astype(bf16)
        tsend[g, 2, 0] = tot[g, 0, left, :].astype(bf16)
        tsend[g, 2, 1] = (tot[g, 1, left, :] + n1[g, 1].astype(f32)).astype(bf16)
        n2_send(g, 0).start()
        n2_send(g, 1).start()

    for d in range(1, 4):
        d_recv(d).wait_recv()
    total_d = rec_d[0] + rec_d[1] + rec_d[2] + rec_d[3]
    for g in range(2):
        for kv in range(2):
            opk_ref[kv, :, g * HD : (g + 1) * HD] = total_d[kv * 2 + g, 0:4, :]

    for g in range(2):
        b = block_of(g)
        n2_send(g, 0).wait_recv()
        n2_send(g, 1).wait_recv()
        for kv in range(2):
            okv_ref[kv, :, g * HD : (g + 1) * HD] = (
                tot[g, kv, rows_of(b), :] + n2[g, 0, kv].astype(f32) + n2[g, 1, kv].astype(f32)
            )

    for g in range(2):
        for k in range(4):
            block_send(g, k).wait_send()
            slab_send(g, k).wait_send()
        for k in range(2):
            m1_send(g, k).wait_send()
            m2_send(g, k).wait_send()
            n1_send(g, k).wait_send()
            n2_send(g, k).wait_send()

    @pl.loop(1, 16)
    def _(d):
        a_send(d).wait_send()
        b_send(d).wait_send()
        c_send(d).wait_send()

    for d in range(1, 4):
        d_send(d).wait_send()


def shards(prompt_kv, comp_q, comp_kv, out_grad, lengths):
    pieces = prompt_kv.reshape(2, 4, 2, HD).transpose(1, 0, 2, 3).reshape(4, 4, HD).astype(f32)
    pieces = jnp.pad(pieces, ((0, 0), (0, 4), (0, 0)))
    vmem = pl.BlockSpec(memory_space=pltpu.VMEM)
    dma = pltpu.SemaphoreType.DMA
    width = comp_q.shape[2]
    out, q_grad, own_grad, prompt_grad = pl.pallas_call(
        kernel,
        out_shape=(
            jax.ShapeDtypeStruct((BLOCK, width), bf16),
            jax.ShapeDtypeStruct((BLOCK, width), bf16),
            jax.ShapeDtypeStruct((2, BLOCK, 2 * HD), f32),
            jax.ShapeDtypeStruct((2, 4, 2 * HD), f32),
        ),
        in_specs=[pl.BlockSpec(memory_space=pltpu.SMEM)] + [vmem] * 4,
        out_specs=[vmem] * 4,
        scratch_shapes=[
            pltpu.VMEM((2, ROWS, HD), bf16),
            pltpu.VMEM((2, ROWS, HD), bf16),
            pltpu.VMEM((2, 4, 2, SLAB, HD), bf16),
            pltpu.VMEM((2, 4, SLAB, ROWS), bf16),
            pltpu.VMEM((2, PROMPT, ROWS), bf16),
            pltpu.VMEM((2, 5, 1, ROWS), f32),
            pltpu.VMEM((2, 1, ROWS), f32),
            pltpu.VMEM((2, 1, ROWS), f32),
            pltpu.VMEM((2, HD, ROWS), f32),
            pltpu.VMEM((2, HD, ROWS), f32),
            pltpu.VMEM((2, 1, ROWS), f32),
            pltpu.VMEM((2, SLAB, HD), f32),
            pltpu.VMEM((2, 3, 2, SLAB, HD), bf16),
            pltpu.VMEM((2, 2, SLAB, HD), f32),
            pltpu.VMEM((2, 2, SLAB, HD), bf16),
            pltpu.VMEM((2, 2, 2, SLAB, HD), bf16),
            pltpu.VMEM((2, 2, SLAB, HD), f32),
            pltpu.VMEM((2, 3, 2, BLOCK, HD), bf16),
            pltpu.VMEM((2, 2, BLOCK, HD), bf16),
            pltpu.VMEM((2, 2, 2, BLOCK, HD), bf16),
            pltpu.VMEM((16 * 8, HD), f32),
            pltpu.VMEM((4, 16, HD), bf16),
            pltpu.VMEM((4, PROMPT, HD), bf16),
            pltpu.VMEM((4, PROMPT, HD), bf16),
            pltpu.VMEM((16, 4, 16, HD), bf16),
            pltpu.VMEM((4, 4, 8, HD), f32),
            pltpu.VMEM((4, 4, 8, HD), f32),
        ]
        + [dma((2, 4))] * 4
        + [dma((2, 2))] * 8
        + [dma((16,))] * 6
        + [dma((4,))] * 2,
        compiler_params=pltpu.CompilerParams(
            collective_id=0, has_side_effects=True, vmem_limit_bytes=56 * 2**20
        ),
    )(lengths, pieces, comp_q[0], comp_kv[:, 0], out_grad[0])
    return out[None], q_grad[None], own_grad[:, None], prompt_grad


def solution(mesh):
    in_specs = (
        P(None, ("roll", "seq", "tp"), None),
        P("roll", "seq", "tp"),
        P(None, "roll", "seq", "tp"),
        P("roll", "seq", "tp"),
        P("roll"),
    )
    out_specs = (
        P("roll", "seq", "tp"),
        P("roll", "seq", "tp"),
        P(None, "roll", "seq", "tp"),
        P(None, ("roll", "seq"), "tp"),
    )
    return jax.shard_map(shards, mesh=mesh, in_specs=in_specs, out_specs=out_specs, check_vma=False)
```

time: 1190 us -> 69.7 us (0.06)
  waiting for transfers between devices: 915 us -> 0 us
  blocking collectives: 180 us -> 0 us
  Pallas kernels: 0 us -> 62.1 us
  local copies, waits for them, and re-layouts: 35 us -> 4.38 us
  other arithmetic: 16.8 us -> 0.61 us
  between operations: 15.5 us -> 1.32 us
  matrix products: 13.2 us -> 0 us
    unnamed x4 -> x0, waiting for transfers between devices: 828 us -> none
    all_gather x1 -> x0, blocking collectives: 180 us -> none  [shards(): lax.all_gather(heads_piece, ('roll', 'seq'), axis=1, tiled=True)]
    reduce_scatter x1 -> x0, waiting for transfers between devices: 84.8 us -> none  [shards(): lax.psum_scatter(own_grads, 'seq', scatter_dimension=2, tiled=True)]
    pallas_call x0 -> x1, Pallas kernels: none -> 62.1 us  [shards(): pl.pallas_call(kernel, out_shape=(jax.ShapeDtypeStruct((BLOCK, width), bf...]
    dot_general x12 -> x0, matrix products: 13.2 us -> none  [the longest x2 3.79 us: grad_advance(): jnp.einsum('kgrd,nkd->kgrn', grad_heads, value_part, preferred_element_ty...]
  transfers between devices with their start and end apart: 4 -> 0, of which waited for: 3 -> 0; matrix products, arithmetic and copies ran while one was open for 2% -> 0% of each run, Pallas kernels for 0% -> 0%
where the time goes in v1:
time: 69.7 us; the launch traced here: 68.4 us
  Pallas kernels  62.1 us (89%)
  local copies, waits for them, and re-layouts  4.38 us (6%)
  between operations  1.32 us (2%)
    pallas_call x1, Pallas kernels, shards(): pl.pallas_call(kernel, out_shape=(jax.ShapeDtypeStruct((BLOCK, width), bf...  62.1 us
    unnamed x12, local copies, waits for them, and re-layouts  4.36 us

profile of v1, /device:TPU:4, one launch (start us, length us, event | category | flops | bytes accessed | tf_op | source)
XLA Modules:
  0.0 68.4 jit_solution(12972298537630484106)
XLA Ops:
  0.6 0.0 copy-start.3
  1.3 0.0 copy-done.3
  1.3 0.6 pad_convert_fusion.pk_ref
  2.0 62.1 %shard_map.84 = (bf16[128,2048]{1,0:T(8,128)(2,1)}, bf16[128,2048]{1,0:T(8,128)(2,1)}, f32[2,128,256]{2,1,0:T(8,128)}, f32[2,4,256]{2,1,0:T(4,128)}) custom-call(s32[1]{0:T(128)S(6)} %copy.15.len_ref, f32[4,8,128]{2,1,0:T(8,128)} %pad_convert_fusion.pk_ref, bf16[128,2048]{1,0:T(8,128)(2,1)} %bitcast.13, bf16[2,128,256]{2,1,0:T(8,128)(2,1)} %bitcast.18, ...), custom_call_target="tpu_custom_call" | custom-call | tf_op jit(solution)/shard_map/pallas_call | solution.py:493
  64.0 0.0 copy-start
  64.0 1.9 %copy.16 = bf16[1,128,2048]{2,1,0:T(8,128)(2,1)} copy(bf16[1,128,2048]{2,1,0:T(8,128)(2,1)} %bitcast.16) | data formatting | bytes 1048576
  66.0 0.0 copy-done
  66.0 0.0 copy-start.1
  66.0 0.8 %copy.17 = bf16[1,128,2048]{2,1,0:T(8,128)(2,1)} copy(bf16[1,128,2048]{2,1,0:T(8,128)(2,1)S(1)} %bitcast.15) | data formatting | bytes 1048576
  66.8 0.3 copy-done.1
  67.1 0.0 copy-start.2
  67.1 0.7 %copy.18 = f32[2,1,128,256]{3,2,1,0:T(8,128)} copy(f32[2,1,128,256]{3,2,1,0:T(8,128)S(1)} %bitcast.17) | data formatting | bytes 524288
  67.8 0.0 copy-done.2
  67.8 0.6 copy.19
  (2 shorter events, 0.0 us)
Async XLA Ops:
  0.6 0.7 %copy-start.3 = (bf16[2,1,1024]{2,0,1:T(2,128)(2,1)S(1)}, bf16[2,1,1024]{2,0,1:T(2,128)(2,1)}, u32[]{:S(2)}) copy-start(bf16[2,1,1024]{2,0,1:T(2,128)(2,1)} %param.5) | copy-start | bytes 12292
  64.0 2.0 %copy-start = (bf16[128,2048]{1,0:T(8,128)(2,1)S(1)}, bf16[128,2048]{1,0:T(8,128)(2,1)}, u32[]{:S(2)}) copy-start(bf16[128,2048]{1,0:T(8,128)(2,1)} %get-tuple-element.9) | copy-start | bytes 1572868
  66.0 1.1 %copy-start.1 = (f32[2,128,256]{2,1,0:T(8,128)S(1)}, f32[2,128,256]{2,1,0:T(8,128)}, u32[]{:S(2)}) copy-start(f32[2,128,256]{2,1,0:T(8,128)} %get-tuple-element.10) | copy-start | bytes 786436
  67.1 0.7 %copy-start.2 = (f32[2,4,256]{2,1,0:T(4,128)S(1)}, f32[2,4,256]{2,1,0:T(4,128)}, u32[]{:S(2)}) copy-start(f32[2,4,256]{2,1,0:T(4,128)} %get-tuple-element.23) | copy-start | bytes 24580

commit v2 on v1

v2 whole, which is shorter than its diff:
```python
import math

import jax
import jax.numpy as jnp
from jax import lax
from jax.experimental import pallas as pl
from jax.experimental.pallas import tpu as pltpu
from jax.sharding import PartitionSpec as P

HD = 128
BLOCK = 128
GROUP = 8
ROWS = GROUP * BLOCK
SLAB = 4 * BLOCK
PROMPT = 256
SCALE = 1.0 / math.sqrt(HD)
LOG2_SCALE = SCALE * math.log2(math.e)
FLOOR = -1e30
f32 = jnp.float32
bf16 = jnp.bfloat16
MESH = pl.DeviceIdType.MESH


def dot_nt(a, b):
    return lax.dot_general(a, b, (((1,), (1,)), ((), ())), preferred_element_type=f32)


def dot_nn(a, b):
    return lax.dot_general(a, b, (((1,), (0,)), ((), ())), preferred_element_type=f32)


def eye(n):
    rows = lax.broadcasted_iota(jnp.int32, (n, n), 0)
    cols = lax.broadcasted_iota(jnp.int32, (n, n), 1)
    return jnp.where(rows == cols, 1.0, 0.0).astype(bf16)


def rem4(i):
    return lax.rem(i, 4)


def kernel(
    len_ref, pk_ref, q_hbm, kv_hbm, do_hbm,
    out_hbm, qg_hbm, okv_hbm, opk_hbm,
    q_ref, kv_ref, do_ref, out_ref, qg_ref, okv_ref, opk_ref,
    qs, dos, kvb, pb, pp, mc, mx, sm, o_t, dq_t, dl, acc,
    part, own, tot, irec, osend, orec,
    buf_s, buf_p, buf_b, pgs, rec_r, src_y, rec_y, src_x, rec_x,
    s_in, r_in, s_out, r_out, s_ri, r_ri, s_ro, r_ro,
    s_p, r_p, s_c, r_c, s_io,
):
    roll = lax.axis_index("roll")
    seq = lax.axis_index("seq")
    tp = lax.axis_index("tp")
    y = lax.div(seq, 4)
    x = rem4(seq)
    length = len_ref[0]
    steps = (1, 3, 2)

    def x_dev(d):
        return {"seq": y * 4 + rem4(x + d)}

    def y_dev(d):
        return {"seq": rem4(y + d) * 4 + x}

    def roll_dev(d):
        return {"roll": rem4(roll + d)}

    def tp_dev(d):
        return {"tp": rem4(tp + d)}

    def inner(g, d):
        return x_dev(d) if g == 0 else y_dev(d)

    def outer(g, d):
        return y_dev(d) if g == 0 else x_dev(d)

    def rcopy(src, dst, ssem, rsem, dev):
        return pltpu.make_async_remote_copy(
            src_ref=src, dst_ref=dst, send_sem=ssem, recv_sem=rsem, device_id=dev, device_id_type=MESH
        )

    def span(i, n):
        return pl.ds(pl.multiple_of(i * n, n), n)

    barrier = pltpu.get_barrier_semaphore()
    for line in (tp_dev, roll_dev, y_dev, x_dev):
        for d in (2, 1, 3):
            pl.semaphore_signal(barrier, inc=1, device_id=line(d), device_id_type=MESH)
    kv_in = pltpu.make_async_copy(kv_hbm, kv_ref, s_io.at[0])
    q_in = pltpu.make_async_copy(q_hbm, q_ref, s_io.at[1])
    do_in = pltpu.make_async_copy(do_hbm, do_ref, s_io.at[2])
    kv_in.start()
    q_in.start()
    do_in.start()

    prompt_row = pk_ref[...].astype(f32)
    pieces = [prompt_row[:, t * HD : (t + 1) * HD] for t in range(8)]
    buf_s[span(seq, 16), :] = jnp.concatenate(pieces, axis=0)
    kv_in.wait()
    for g in range(2):
        for kv in range(2):
            kvb[g, 0, kv, :BLOCK, :] = kv_ref[kv, :, g * HD : (g + 1) * HD]

    for p in range(1, 4):

        @pl.when(y + p < 4)
        def _():
            kvb[1, :, :, p * BLOCK : (p + 1) * BLOCK, :] = jnp.zeros((4, 2, BLOCK, HD), bf16)

    pl.semaphore_wait(barrier, 12)

    def seen_slab(g, e, act):
        if g == 0 and e > 0:
            pl.when(y + e >= 4)(act)
        else:
            act()

    def outer_copy(g, k):
        d = steps[k]
        src = kvb.at[g, 0, :, :BLOCK, :]
        return rcopy(src, kvb.at[g, 4 - d, :, :BLOCK, :], s_out.at[g, k], r_out.at[g, k], outer(g, d))

    def outer_start(g, k):
        def act():
            outer_copy(g, k).start()

        pl.when(y + steps[k] < 4)(act) if g == 0 else act()

    def inner_copy(g, e, k):
        d = steps[k]
        src = kvb.at[g, e, :, :BLOCK, :]
        dst = kvb.at[g, e, :, (4 - d) * BLOCK : (5 - d) * BLOCK, :]
        return rcopy(src, dst, s_in.at[g, e, k], r_in.at[g, e, k], inner(g, d))

    def inner_do(g, e, sends, act):
        def each():
            for k in range(3):
                if g == 0:
                    act(k)
                else:
                    pl.when(y + steps[k] < 4 if sends else y >= steps[k])(lambda: act(k))

        seen_slab(g, e, each)

    def inner_start(g, e):
        inner_do(g, e, True, lambda k: inner_copy(g, e, k).start())

    def inner_wait(g, e):
        inner_do(g, e, False, lambda k: inner_copy(g, e, k).wait_recv())

    def px_copy(k, from_offset):
        ref = buf_s.at[span(y * 4 + rem4(x + from_offset), 16), :]
        return rcopy(ref, ref, s_p.at[0, k], r_p.at[0, k], x_dev(steps[k]))

    def py_copy(k, from_offset):
        ref = buf_s.at[span(rem4(y + from_offset), 64), :]
        return rcopy(ref, ref, s_p.at[1, k], r_p.at[1, k], y_dev(steps[k]))

    def tp_copy(k, from_offset):
        dst = buf_b.at[:, span(roll * 4 + rem4(tp + from_offset), 16), :]
        return rcopy(buf_p.at[rem4(tp + steps[k])], dst, s_p.at[2, k], r_p.at[2, k], tp_dev(steps[k]))

    def roll_copy(k, from_offset):
        ref = buf_b.at[:, span(rem4(roll + from_offset), 64), :]
        return rcopy(ref, ref, s_p.at[3, k], r_p.at[3, k], roll_dev(steps[k]))

    prompt_copies = (px_copy, py_copy, tp_copy, roll_copy)

    def prompt_start(stage):
        for k in range(3):
            prompt_copies[stage](k, 0).start()

    def prompt_wait(stage):
        for k in range(3):
            prompt_copies[stage](k, 4 - steps[k]).wait_recv()

    for k in range(3):
        for g in range(2):
            outer_start(g, k)
    prompt_start(0)
    for g in range(2):
        inner_start(g, 0)

    q_in.wait()
    do_in.wait()
    live_rows = seq * BLOCK + lax.broadcasted_iota(jnp.int32, (BLOCK, HD), 0) < length
    for g in range(2):
        for h in range(GROUP):
            cols = slice((g * GROUP + h) * HD, (g * GROUP + h + 1) * HD)
            rows = slice(h * BLOCK, (h + 1) * BLOCK)
            qs[g, rows, :] = q_ref[:, cols]
            dos[g, rows, :] = jnp.where(live_rows, do_ref[:, cols].astype(f32), 0.0).astype(bf16)
    mx[...] = jnp.full(mx.shape, FLOOR, f32)
    sm[...] = jnp.zeros(sm.shape, f32)
    o_t[...] = jnp.zeros(o_t.shape, f32)
    dq_t[...] = jnp.zeros(dq_t.shape, f32)

    prompt_wait(0)
    prompt_start(1)
    for k in range(3):
        for g in range(2):
            e = 4 - steps[k]
            seen_slab(g, e, lambda: outer_copy(g, k).wait_recv())
            inner_start(g, e)

    def fwd(g, c, k, v, p_ref, mask):
        n = k.shape[0]
        v_t = dot_nt(eye(HD), v).astype(bf16)
        s = dot_nt(k, qs[g]) * LOG2_SCALE
        if mask is not None:
            s = jnp.where(mask(n), s, FLOOR)
        m_old = mx[g]
        m_new = jnp.maximum(m_old, jnp.max(s, axis=0, keepdims=True))
        p = jnp.exp2(s - m_new)
        alpha = jnp.exp2(m_old - m_new)
        mx[g] = m_new
        mc[g, c] = m_new
        sm[g] = sm[g] * alpha + jnp.sum(p, axis=0, keepdims=True)
        rounded = p.astype(bf16)
        p_ref[...] = rounded
        o_t[g] = o_t[g] * alpha + dot_nn(v_t, rounded)

    def fwd_slab(g, e):
        none_seen = (g == 0) & (e > 0) & (y + e < 4)
        all_seen = jnp.where(g == 0, y + e >= 4, (y == 3) & (x + e >= 4))

        def mask(n):
            row = lax.broadcasted_iota(jnp.int32, (n, 1), 0)
            block = lax.div(row, BLOCK)
            key_y = rem4(y + jnp.where(g == 0, e, block))
            key_x = rem4(x + jnp.where(g == 0, block, e))
            key_block = key_y * 4 + key_x
            key_pos = key_block * BLOCK + lax.rem(row, BLOCK)
            lane = lax.broadcasted_iota(jnp.int32, (1, ROWS), 1)
            return key_pos <= seq * BLOCK + lax.rem(lane, BLOCK)

        @pl.when(all_seen)
        def _():
            fwd(g, e, kvb[g, e, 0], kvb[g, e, 1], pb.at[g, e], None)

        @pl.when(jnp.logical_not(all_seen | none_seen))
        def _():
            fwd(g, e, kvb[g, e, 0], kvb[g, e, 1], pb.at[g, e], mask)

    @pl.loop(0, 10)
    def _(i):
        g = lax.rem(i, 2)
        kind = lax.div(i, 2)

        for h in range(2):
            for k, e in enumerate((0, 3, 1, 2)):

                @pl.when(i == 2 * k + h)
                def _():
                    inner_wait(h, e)

        @pl.when(i == 2)
        def _():
            prompt_wait(1)
            for t in range(4):
                for j in range(4):
                    buf_p[t, j] = buf_s[pl.ds(t * 4 + j, 16, stride=16), :].astype(bf16)
            prompt_start(2)
            buf_b[:, span(roll * 4 + tp, 16), :] = buf_p[tp]

        @pl.when(i == 5)
        def _():
            prompt_wait(2)
            prompt_start(3)

        @pl.when(i == 8)
        def _():
            prompt_wait(3)

        @pl.when(kind == 4)
        def _():
            fwd(g, 4, buf_b[g * 2], buf_b[g * 2 + 1], pp.at[g], None)

        @pl.when(kind != 4)
        def _():
            fwd_slab(g, jnp.where(kind == 1, 3, jnp.where(kind == 2, 1, jnp.where(kind == 3, 2, 0))))

    @pl.loop(0, 2)
    def _(g):
        inv = 1.0 / sm[g]
        mixed = o_t[g] * inv
        dl[g] = jnp.sum(dot_nt(eye(HD), dos[g]) * mixed, axis=0, keepdims=True)
        sm[g] = inv
        lane = lax.broadcasted_iota(jnp.int32, (1, ROWS), 1)
        live = seq * BLOCK + lax.rem(lane, BLOCK) < length
        rounded = jnp.where(live, mixed, 0.0).astype(bf16)
        for h in range(GROUP):
            head = dot_nt(eye(BLOCK), rounded[:, h * BLOCK : (h + 1) * BLOCK])
            out_ref[:, span(g * GROUP + h, HD)] = head.astype(bf16)

    out_done = pltpu.make_async_copy(out_ref, out_hbm, s_io.at[3])
    out_done.start()

    def bwd(g, c, k, v, p):
        n = k.shape[0]
        k_t = dot_nt(eye(HD), k).astype(bf16)
        factor = jnp.exp2(mc[g, c] - mx[g]) * sm[g]
        dp = dot_nt(v, dos[g])
        w = p.astype(f32) * factor
        ds = (w * (dp - dl[g])).astype(bf16)
        acc[1, :n] = dot_nn(w.astype(bf16), dos[g])
        acc[0, :n] = dot_nn(ds, qs[g]) * SCALE
        dq_t[g] += dot_nn(k_t, ds)

    def ri_copy(g, e, k):
        d = steps[k]
        src = part.at[g, e, :, d * BLOCK : (d + 1) * BLOCK, :]
        return rcopy(src, irec.at[g, e, k], s_ri.at[g, e, k], r_ri.at[g, e, k], inner(g, d))

    def ri_do(g, e, sends, act):
        def each():
            for k in range(3):
                if g == 0:
                    act(k)
                else:
                    pl.when(y + steps[k] >= 4 if sends else y < steps[k])(lambda: act(k))

        seen_slab(g, e, each)

    def ri_start(g, e):
        ri_do(g, e, True, lambda k: ri_copy(g, e, k).start())

    def ro_copy(g, e):
        return rcopy(osend.at[g, e], orec.at[g, e], s_ro.at[g, e], r_ro.at[g, e], outer(g, e))

    def ro_start(g, e):
        def act():
            own[g] = part[g, e, :, :BLOCK, :].astype(f32)

            def add(k):
                ri_copy(g, e, k).wait_recv()
                own[g] += irec[g, e, k].astype(f32)

            ri_do(g, e, False, add)
            osend[g, e] = own[g].astype(bf16)
            ro_copy(g, e).start()

        seen_slab(g, e, act)

    def cr_copy(k, from_offset):
        src = pgs.at[:, span(rem4(roll + steps[k]), 64), :]
        return rcopy(src, rec_r.at[rem4(roll + from_offset)], s_c.at[0, k], r_c.at[0, k], roll_dev(steps[k]))

    def cy_copy(k, from_offset):
        src = src_y.at[rem4(y + steps[k])]
        return rcopy(src, rec_y.at[rem4(y + from_offset)], s_c.at[1, k], r_c.at[1, k], y_dev(steps[k]))

    def cx_copy(k, from_offset):
        src = src_x.at[rem4(x + steps[k])]
        return rcopy(src, rec_x.at[rem4(x + from_offset)], s_c.at[2, k], r_c.at[2, k], x_dev(steps[k]))

    sum_copies = (cr_copy, cy_copy, cx_copy)

    def sum_start(stage):
        for k in range(3):
            sum_copies[stage](k, 0).start()

    def sum_wait(stage):
        for k in range(3):
            sum_copies[stage](k, 4 - steps[k]).wait_recv()

    def total4(ref):
        return (ref[0].astype(f32) + ref[1].astype(f32)) + (ref[2].astype(f32) + ref[3].astype(f32))

    @pl.loop(0, 10)
    def _(i):
        g = lax.rem(i, 2)
        kind = lax.div(i, 2)
        e = jnp.where(kind == 1, 2, jnp.where(kind == 2, 1, jnp.where(kind == 3, 3, 0)))
        none_seen = (g == 0) & (e > 0) & (y + e < 4)

        @pl.when(i == 5)
        def _():
            sum_wait(0)
            total_r = total4(rec_r)
            for r in range(4):
                rows = [total_r[:, t * 16 + r * 4 : t * 16 + r * 4 + 4, :] for t in range(4)]
                src_y[r] = jnp.concatenate(rows, axis=1).astype(bf16)
            sum_start(1)
            rec_y[y] = src_y[y]

        for h in range(2):

            @pl.when(i == 7 + h)
            def _():
                ro_start(h, 2)

        @pl.when(i == 9)
        def _():
            ro_start(0, 1)
            sum_wait(1)
            total_y = total4(rec_y)
            for r in range(4):
                rows = [total_y[:, t * 4 + r : t * 4 + r + 1, :] for t in range(4)]
                src_x[r] = jnp.concatenate(rows + rows, axis=1)
            sum_start(2)
            rec_x[x] = src_x[x]

        @pl.when(kind == 0)
        def _():
            bwd(g, 4, buf_b[g * 2], buf_b[g * 2 + 1], pp[g])
            pgs[g * 2] = acc[0, :PROMPT].astype(bf16)
            pgs[g * 2 + 1] = acc[1, :PROMPT].astype(bf16)

        @pl.when((kind != 0) & jnp.logical_not(none_seen))
        def _():
            bwd(g, e, kvb[g, e, 0], kvb[g, e, 1], pb[g, e])
            part[g, e] = acc[...].astype(bf16)

        @pl.when(kind == 4)
        def _():
            tot[g] = acc[:, :BLOCK, :]

        for h in range(2):
            for k, ahead in enumerate((None, 2, 1, 3, 0)):
                if ahead is not None:

                    @pl.when(i == 2 * k + h)
                    def _():
                        ri_start(h, ahead)

        @pl.when(i == 1)
        def _():
            sum_start(0)
            rec_r[roll] = pgs[:, span(roll, 64), :]

    ro_start(1, 1)
    for g in range(2):
        ro_start(g, 3)

    @pl.loop(0, 2)
    def _(g):
        rounded = (dq_t[g] * SCALE).astype(bf16)
        for h in range(GROUP):
            head = dot_nt(eye(BLOCK), rounded[:, h * BLOCK : (h + 1) * BLOCK])
            qg_ref[:, span(g * GROUP + h, HD)] = head.astype(bf16)

    qg_done = pltpu.make_async_copy(qg_ref, qg_hbm, s_io.at[4])
    qg_done.start()

    for g in range(2):

        def add_inner(k):
            ri_copy(g, 0, k).wait_recv()
            tot[g] += irec[g, 0, k].astype(f32)

        ri_do(g, 0, False, add_inner)
        for e in (2, 1, 3):

            def add_outer():
                ro_copy(g, e).wait_recv()
                tot[g] += orec[g, e].astype(f32)

            pl.when(y < e)(add_outer) if g == 0 else add_outer()
        for kv in range(2):
            okv_ref[kv, :, g * HD : (g + 1) * HD] = tot[g, kv]
    okv_done = pltpu.make_async_copy(okv_ref, okv_hbm, s_io.at[5])
    okv_done.start()

    sum_wait(2)
    total_d = total4(rec_x)
    for g in range(2):
        for kv in range(2):
            opk_ref[kv, :, g * HD : (g + 1) * HD] = total_d[g * 2 + kv, 0:4, :]
    opk_done = pltpu.make_async_copy(opk_ref, opk_hbm, s_io.at[6])
    opk_done.start()

    for g in range(2):
        for e in range(4):
            inner_do(g, e, True, lambda k: inner_copy(g, e, k).wait_send())
            ri_do(g, e, True, lambda k: ri_copy(g, e, k).wait_send())
            if e > 0:
                seen_slab(g, e, lambda: ro_copy(g, e).wait_send())
        for k in range(3):
            pl.when(y + steps[k] < 4)(lambda: outer_copy(g, k).wait_send()) if g == 0 else outer_copy(g, k).wait_send()
    for k in range(3):
        for copy in prompt_copies + sum_copies:
            copy(k, 0).wait_send()
    out_done.wait()
    qg_done.wait()
    okv_done.wait()
    opk_done.wait()


def store_kernel(a, b, c, d, a_out, b_out, c_out, d_out, sems):
    pairs = ((a, a_out), (b, b_out), (c, c_out), (d, d_out))
    copies = [pltpu.make_async_copy(src, dst, sems.at[i]) for i, (src, dst) in enumerate(pairs)]
    for copy in copies:
        copy.start()
    for copy in copies:
        copy.wait()


def shards(prompt_kv, comp_q, comp_kv, out_grad, lengths):
    vmem = pl.BlockSpec(memory_space=pltpu.VMEM)
    anywhere = pl.BlockSpec(memory_space=pl.ANY)
    dma = pltpu.SemaphoreType.DMA
    width = comp_q.shape[2]
    out_shape = (
        jax.ShapeDtypeStruct((BLOCK, width), bf16),
        jax.ShapeDtypeStruct((BLOCK, width), bf16),
        jax.ShapeDtypeStruct((2, BLOCK, 2 * HD), f32),
        jax.ShapeDtypeStruct((2, 4, 2 * HD), f32),
    )
    results = pl.pallas_call(
        kernel,
        out_shape=out_shape,
        in_specs=[pl.BlockSpec(memory_space=pltpu.SMEM), vmem] + [anywhere] * 3,
        out_specs=[anywhere] * 4,
        scratch_shapes=[
            pltpu.VMEM((BLOCK, width), bf16),
            pltpu.VMEM((2, BLOCK, 2 * HD), bf16),
            pltpu.VMEM((BLOCK, width), bf16),
            pltpu.VMEM((BLOCK, width), bf16),
            pltpu.VMEM((BLOCK, width), bf16),
            pltpu.VMEM((2, BLOCK, 2 * HD), f32),
            pltpu.VMEM((2, 4, 2 * HD), f32),
            pltpu.VMEM((2, ROWS, HD), bf16),
            pltpu.VMEM((2, ROWS, HD), bf16),
            pltpu.VMEM((2, 4, 2, SLAB, HD), bf16),
            pltpu.VMEM((2, 4, SLAB, ROWS), bf16),
            pltpu.VMEM((2, PROMPT, ROWS), bf16),
            pltpu.VMEM((2, 5, 1, ROWS), f32),
            pltpu.VMEM((2, 1, ROWS), f32),
            pltpu.VMEM((2, 1, ROWS), f32),
            pltpu.VMEM((2, HD, ROWS), f32),
            pltpu.VMEM((2, HD, ROWS), f32),
            pltpu.VMEM((2, 1, ROWS), f32),
            pltpu.VMEM((2, SLAB, HD), f32),
            pltpu.VMEM((2, 4, 2, SLAB, HD), bf16),
            pltpu.VMEM((2, 2, BLOCK, HD), f32),
            pltpu.VMEM((2, 2, BLOCK, HD), f32),
            pltpu.VMEM((2, 4, 3, 2, BLOCK, HD), bf16),
            pltpu.VMEM((2, 4, 2, BLOCK, HD), bf16),
            pltpu.VMEM((2, 4, 2, BLOCK, HD), bf16),
            pltpu.VMEM((16 * 16, HD), f32),
            pltpu.VMEM((4, 4, 16, HD), bf16),
            pltpu.VMEM((4, PROMPT, HD), bf16),
            pltpu.VMEM((4, PROMPT, HD), bf16),
            pltpu.VMEM((4, 4, 64, HD), bf16),
            pltpu.VMEM((4, 4, 16, HD), bf16),
            pltpu.VMEM((4, 4, 16, HD), bf16),
            pltpu.VMEM((4, 4, 8, HD), f32),
            pltpu.VMEM((4, 4, 8, HD), f32),
        ]
        + ([dma((2, 4, 3))] * 2 + [dma((2, 3))] * 2)
        + ([dma((2, 4, 3))] * 2 + [dma((2, 4))] * 2)
        + [dma((4, 3))] * 2
        + [dma((3, 3))] * 2
        + [dma((7,))],
        compiler_params=pltpu.CompilerParams(
            collective_id=0, has_side_effects=True, vmem_limit_bytes=56 * 2**20
        ),
    )(lengths, prompt_kv[:, 0], comp_q[0], comp_kv[:, 0], out_grad[0])
    out, q_grad, own_grad, prompt_grad = pl.pallas_call(
        store_kernel,
        out_shape=out_shape,
        in_specs=[vmem] * 4,
        out_specs=[anywhere] * 4,
        scratch_shapes=[dma((4,))],
    )(*results)
    return out[None], q_grad[None], own_grad[:, None], prompt_grad


def solution(mesh):
    in_specs = (
        P(None, ("roll", "seq", "tp"), None),
        P("roll", "seq", "tp"),
        P(None, "roll", "seq", "tp"),
        P("roll", "seq", "tp"),
        P("roll"),
    )
    out_specs = (
        P("roll", "seq", "tp"),
        P("roll", "seq", "tp"),
        P(None, "roll", "seq", "tp"),
        P(None, ("roll", "seq"), "tp"),
    )
    return jax.shard_map(shards, mesh=mesh, in_specs=in_specs, out_specs=out_specs, check_vma=False)
```

time: 69.7 us -> 65.4 us (0.938)
  local copies, waits for them, and re-layouts: 4.38 us -> 0 us
  Pallas kernels: 62.1 us -> 63.2 us
    unnamed x12 -> x0, local copies, waits for them, and re-layouts: 4.36 us -> none
    pallas_call x1 -> x2, Pallas kernels: 62.1 us -> 63.2 us  [the longest x1 60.8 us: shards(): pl.pallas_call(kernel, out_shape=out_shape, in_specs=[pl.BlockSpec(memory...]
where the time goes in v2:
time: 65.4 us; the launch traced here: 64.4 us
  Pallas kernels  63.2 us (97%)
  between operations  1.29 us (2%)
    pallas_call x1, Pallas kernels, shards(): pl.pallas_call(kernel, out_shape=out_shape, in_specs=[pl.BlockSpec(memory...  60.8 us
    pallas_call x1, Pallas kernels, shards(): pl.pallas_call(store_kernel, out_shape=out_shape, in_specs=[vmem] * 4, ou...  2.35 us

profile of v2, /device:TPU:4, one launch (start us, length us, event | category | flops | bytes accessed | tf_op | source)
XLA Modules:
  0.0 64.4 jit_solution(16276448203108508649)
XLA Ops:
  1.3 60.8 %shard_map.84 = (bf16[128,2048]{1,0:T(8,128)(2,1)}, bf16[128,2048]{1,0:T(8,128)(2,1)}, f32[2,128,256]{2,1,0:T(8,128)}, f32[2,4,256]{2,1,0:T(4,128)}) custom-call(s32[1]{0:T(128)S(6)} %copy.10.len_ref, bf16[2,1024]{1,0:T(2,128)(2,1)} %bitcast.12, bf16[128,2048]{1,0:T(8,128)(2,1)} %bitcast.9, bf16[2,128,256]{2,1,0:T(8,128)(2,1)} %bitcast.11, ...), custom_call_target="tpu_custom_call" | custom-call | tf_op jit(solution)/shard_map/pallas_call | solution.py:511
  62.1 2.4 %shard_map.85 = (bf16[128,2048]{1,0:T(8,128)(2,1)}, bf16[128,2048]{1,0:T(8,128)(2,1)}, f32[2,128,256]{2,1,0:T(8,128)}, f32[2,4,256]{2,1,0:T(4,128)}) custom-call(bf16[128,2048]{1,0:T(8,128)(2,1)} %get-tuple-element.12.a, bf16[128,2048]{1,0:T(8,128)(2,1)} %get-tuple-element.13.b, f32[2,128,256]{2,1,0:T(8,128)} %get-tuple-element.14.c, ...), custom_call_target="tpu_custom_call" | custom-call | tf_op jit(solution)/shard_map/pallas_call | solution.py:561

commit v3 on v2

--- a/solution.py
+++ b/solution.py
@@ -45,7 +45,7 @@
     q_ref, kv_ref, do_ref, out_ref, qg_ref, okv_ref, opk_ref,
     qs, dos, kvb, pb, pp, mc, mx, sm, o_t, dq_t, dl, acc,
     part, own, tot, irec, osend, orec,
-    buf_s, buf_p, buf_b, pgs, rec_r, src_y, rec_y, src_x, rec_x,
+    buf_s, src_t, rec_t, buf_b, pgs, rec_y, src_r, rec_r, src_x, rec_x,
     s_in, r_in, s_out, r_out, s_ri, r_ri, s_ro, r_ro,
     s_p, r_p, s_c, r_c, s_io,
 ):
@@ -96,7 +96,7 @@
 
     prompt_row = pk_ref[...].astype(f32)
     pieces = [prompt_row[:, t * HD : (t + 1) * HD] for t in range(8)]
-    buf_s[span(seq, 16), :] = jnp.concatenate(pieces, axis=0)
+    buf_s[span(x, 16), :] = jnp.concatenate(pieces, axis=0)
     kv_in.wait()
     for g in range(2):
         for kv in range(2):
@@ -107,6 +107,10 @@
         @pl.when(y + p < 4)
         def _():
             kvb[1, :, :, p * BLOCK : (p + 1) * BLOCK, :] = jnp.zeros((4, 2, BLOCK, HD), bf16)
+
+        @pl.when(x + p < 4)
+        def _():
+            kvb[0, 0, :, p * BLOCK : (p + 1) * BLOCK, :] = jnp.zeros((2, BLOCK, HD), bf16)
 
     pl.semaphore_wait(barrier, 12)
 
@@ -136,10 +140,11 @@
     def inner_do(g, e, sends, act):
         def each():
             for k in range(3):
-                if g == 0:
+                at = x if g == 0 else y
+                if g == 0 and e > 0:
                     act(k)
                 else:
-                    pl.when(y + steps[k] < 4 if sends else y >= steps[k])(lambda: act(k))
+                    pl.when(at + steps[k] < 4 if sends else at >= steps[k])(lambda: act(k))
 
         seen_slab(g, e, each)
 
@@ -150,22 +155,22 @@
         inner_do(g, e, False, lambda k: inner_copy(g, e, k).wait_recv())
 
     def px_copy(k, from_offset):
-        ref = buf_s.at[span(y * 4 + rem4(x + from_offset), 16), :]
+        ref = buf_s.at[span(rem4(x + from_offset), 16), :]
         return rcopy(ref, ref, s_p.at[0, k], r_p.at[0, k], x_dev(steps[k]))
 
+    def tp_copy(k, from_offset):
+        dst = rec_t.at[rem4(tp + from_offset)]
+        return rcopy(src_t.at[rem4(tp + steps[k])], dst, s_p.at[1, k], r_p.at[1, k], tp_dev(steps[k]))
+
+    def roll_copy(k, from_offset):
+        ref = buf_b.at[:, span(y * 4 + rem4(roll + from_offset), 16), :]
+        return rcopy(ref, ref, s_p.at[2, k], r_p.at[2, k], roll_dev(steps[k]))
+
     def py_copy(k, from_offset):
-        ref = buf_s.at[span(rem4(y + from_offset), 64), :]
-        return rcopy(ref, ref, s_p.at[1, k], r_p.at[1, k], y_dev(steps[k]))
-
-    def tp_copy(k, from_offset):
-        dst = buf_b.at[:, span(roll * 4 + rem4(tp + from_offset), 16), :]
-        return rcopy(buf_p.at[rem4(tp + steps[k])], dst, s_p.at[2, k], r_p.at[2, k], tp_dev(steps[k]))
-
-    def roll_copy(k, from_offset):
-        ref = buf_b.at[:, span(rem4(roll + from_offset), 64), :]
-        return rcopy(ref, ref, s_p.at[3, k], r_p.at[3, k], roll_dev(steps[k]))
-
-    prompt_copies = (px_copy, py_copy, tp_copy, roll_copy)
+        ref = buf_b.at[:, span(rem4(y + from_offset), 64), :]
+        return rcopy(ref, ref, s_p.at[3, k], r_p.at[3, k], y_dev(steps[k]))
+
+    prompt_copies = (px_copy, tp_copy, roll_copy, py_copy)
 
     def prompt_start(stage):
         for k in range(3):
@@ -197,12 +202,20 @@
     dq_t[...] = jnp.zeros(dq_t.shape, f32)
 
     prompt_wait(0)
+    for t in range(4):
+        for j in range(4):
+            rows = buf_s[pl.ds(t * 4 + j, 4, stride=16), :]
+            src_t[t, j] = jnp.concatenate([rows, rows], axis=0)
     prompt_start(1)
-    for k in range(3):
+    rec_t[tp] = src_t[tp]
+    def pass_on(k):
         for g in range(2):
             e = 4 - steps[k]
             seen_slab(g, e, lambda: outer_copy(g, k).wait_recv())
             inner_start(g, e)
+
+    pass_on(0)
+    pass_on(1)
 
     def fwd(g, c, k, v, p_ref, mask):
         n = k.shape[0]
@@ -255,16 +268,16 @@
                 def _():
                     inner_wait(h, e)
 
-        @pl.when(i == 2)
-        def _():
+        @pl.when(i == 1)
+        def _():
+            pass_on(2)
             prompt_wait(1)
-            for t in range(4):
-                for j in range(4):
-                    buf_p[t, j] = buf_s[pl.ds(t * 4 + j, 16, stride=16), :].astype(bf16)
+            for j in range(4):
+                rows = [rec_t[t, j, 0:4, :] for t in range(4)]
+                buf_b[j, span(y * 4 + roll, 16), :] = jnp.concatenate(rows, axis=0).astype(bf16)
             prompt_start(2)
-            buf_b[:, span(roll * 4 + tp, 16), :] = buf_p[tp]
-
-        @pl.when(i == 5)
+
+        @pl.when(i == 4)
         def _():
             prompt_wait(2)
             prompt_start(3)
@@ -316,10 +329,11 @@
     def ri_do(g, e, sends, act):
         def each():
             for k in range(3):
-                if g == 0:
+                at = x if g == 0 else y
+                if g == 0 and e > 0:
                     act(k)
                 else:
-                    pl.when(y + steps[k] >= 4 if sends else y < steps[k])(lambda: act(k))
+                    pl.when(at + steps[k] >= 4 if sends else at < steps[k])(lambda: act(k))
 
         seen_slab(g, e, each)
 
@@ -343,19 +357,19 @@
 
         seen_slab(g, e, act)
 
+    def cy_copy(k, from_offset):
+        src = pgs.at[:, span(rem4(y + steps[k]), 64), :]
+        return rcopy(src, rec_y.at[rem4(y + from_offset)], s_c.at[0, k], r_c.at[0, k], y_dev(steps[k]))
+
     def cr_copy(k, from_offset):
-        src = pgs.at[:, span(rem4(roll + steps[k]), 64), :]
-        return rcopy(src, rec_r.at[rem4(roll + from_offset)], s_c.at[0, k], r_c.at[0, k], roll_dev(steps[k]))
-
-    def cy_copy(k, from_offset):
-        src = src_y.at[rem4(y + steps[k])]
-        return rcopy(src, rec_y.at[rem4(y + from_offset)], s_c.at[1, k], r_c.at[1, k], y_dev(steps[k]))
+        src = src_r.at[:, span(rem4(roll + steps[k]), 16), :]
+        return rcopy(src, rec_r.at[rem4(roll + from_offset)], s_c.at[1, k], r_c.at[1, k], roll_dev(steps[k]))
 
     def cx_copy(k, from_offset):
         src = src_x.at[rem4(x + steps[k])]
         return rcopy(src, rec_x.at[rem4(x + from_offset)], s_c.at[2, k], r_c.at[2, k], x_dev(steps[k]))
 
-    sum_copies = (cr_copy, cy_copy, cx_copy)
+    sum_copies = (cy_copy, cr_copy, cx_copy)
 
     def sum_start(stage):
         for k in range(3):
@@ -378,12 +392,9 @@
         @pl.when(i == 5)
         def _():
             sum_wait(0)
-            total_r = total4(rec_r)
-            for r in range(4):
-                rows = [total_r[:, t * 16 + r * 4 : t * 16 + r * 4 + 4, :] for t in range(4)]
-                src_y[r] = jnp.concatenate(rows, axis=1).astype(bf16)
+            src_r[...] = total4(rec_y).astype(bf16)
             sum_start(1)
-            rec_y[y] = src_y[y]
+            rec_r[roll] = src_r[:, span(roll, 16), :]
 
         for h in range(2):
 
@@ -395,9 +406,9 @@
         def _():
             ro_start(0, 1)
             sum_wait(1)
-            total_y = total4(rec_y)
+            total_r = total4(rec_r)
             for r in range(4):
-                rows = [total_y[:, t * 4 + r : t * 4 + r + 1, :] for t in range(4)]
+                rows = [total_r[:, t * 4 + r : t * 4 + r + 1, :] for t in range(4)]
                 src_x[r] = jnp.concatenate(rows + rows, axis=1)
             sum_start(2)
             rec_x[x] = src_x[x]
@@ -428,11 +439,10 @@
         @pl.when(i == 1)
         def _():
             sum_start(0)
-            rec_r[roll] = pgs[:, span(roll, 64), :]
+            rec_y[y] = pgs[:, span(y, 64), :]
 
     ro_start(1, 1)
-    for g in range(2):
-        ro_start(g, 3)
+    ro_start(0, 3)
 
     @pl.loop(0, 2)
     def _(g):
@@ -441,6 +451,7 @@
             head = dot_nt(eye(BLOCK), rounded[:, h * BLOCK : (h + 1) * BLOCK])
             qg_ref[:, span(g * GROUP + h, HD)] = head.astype(bf16)
 
+    ro_start(1, 3)
     qg_done = pltpu.make_async_copy(qg_ref, qg_hbm, s_io.at[4])
     qg_done.start()
 
@@ -539,12 +550,13 @@
             pltpu.VMEM((2, 4, 3, 2, BLOCK, HD), bf16),
             pltpu.VMEM((2, 4, 2, BLOCK, HD), bf16),
             pltpu.VMEM((2, 4, 2, BLOCK, HD), bf16),
-            pltpu.VMEM((16 * 16, HD), f32),
-            pltpu.VMEM((4, 4, 16, HD), bf16),
+            pltpu.VMEM((4 * 16, HD), f32),
+            pltpu.VMEM((4, 4, 8, HD), f32),
+            pltpu.VMEM((4, 4, 8, HD), f32),
             pltpu.VMEM((4, PROMPT, HD), bf16),
             pltpu.VMEM((4, PROMPT, HD), bf16),
             pltpu.VMEM((4, 4, 64, HD), bf16),
-            pltpu.VMEM((4, 4, 16, HD), bf16),
+            pltpu.VMEM((4, 64, HD), bf16),
             pltpu.VMEM((4, 4, 16, HD), bf16),
             pltpu.VMEM((4, 4, 8, HD), f32),
             pltpu.VMEM((4, 4, 8, HD), f32),

time: 65.4 us -> 60.8 us (0.930); the launches traced: 64.4 us -> 60.6 us
  Pallas kernels: 63.2 us -> 59.3 us
    pallas_call x1, Pallas kernels: 60.8 us -> 57 us  [shards(): pl.pallas_call(kernel, out_shape=out_shape, in_specs=[pl.BlockSpec(memory...]
where the time goes in v3:
time: 60.8 us; the launch traced here: 60.6 us
  Pallas kernels  59.3 us (98%)
  between operations  1.29 us (2%)
    pallas_call x1, Pallas kernels, shards(): pl.pallas_call(kernel, out_shape=out_shape, in_specs=[pl.BlockSpec(memory...  57 us
    pallas_call x1, Pallas kernels, shards(): pl.pallas_call(store_kernel, out_shape=out_shape, in_specs=[vmem] * 4, ou...  2.35 us

profile of v3, /device:TPU:4, one launch (start us, length us, event | category | flops | bytes accessed | tf_op | source)
XLA Modules:
  0.0 60.6 jit_solution(5018853769089116953)
XLA Ops:
  1.3 57.0 %shard_map.84 = (bf16[128,2048]{1,0:T(8,128)(2,1)}, bf16[128,2048]{1,0:T(8,128)(2,1)}, f32[2,128,256]{2,1,0:T(8,128)}, f32[2,4,256]{2,1,0:T(4,128)}) custom-call(s32[1]{0:T(128)S(6)} %copy.10.len_ref, bf16[2,1024]{1,0:T(2,128)(2,1)} %bitcast.12, bf16[128,2048]{1,0:T(8,128)(2,1)} %bitcast.9, bf16[2,128,256]{2,1,0:T(8,128)(2,1)} %bitcast.11, ...), custom_call_target="tpu_custom_call" | custom-call | tf_op jit(solution)/shard_map/pallas_call | solution.py:522
  58.3 2.4 %shard_map.85 = (bf16[128,2048]{1,0:T(8,128)(2,1)}, bf16[128,2048]{1,0:T(8,128)(2,1)}, f32[2,128,256]{2,1,0:T(8,128)}, f32[2,4,256]{2,1,0:T(4,128)}) custom-call(bf16[128,2048]{1,0:T(8,128)(2,1)} %get-tuple-element.12.a, bf16[128,2048]{1,0:T(8,128)(2,1)} %get-tuple-element.13.b, f32[2,128,256]{2,1,0:T(8,128)} %get-tuple-element.14.c, ...), custom_call_target="tpu_custom_call" | custom-call | tf_op jit(solution)/shard_map/pallas_call | solution.py:573

commit v4 on v3

--- a/solution.py
+++ b/solution.py
@@ -43,7 +43,7 @@
     len_ref, pk_ref, q_hbm, kv_hbm, do_hbm,
     out_hbm, qg_hbm, okv_hbm, opk_hbm,
     q_ref, kv_ref, do_ref, out_ref, qg_ref, okv_ref, opk_ref,
-    qs, dos, kvb, pb, pp, mc, mx, sm, o_t, dq_t, dl, acc,
+    qs, dos, kvb, pb, pp, mc, mx, sm, o_t, dq_t, dl, do_t,
     part, own, tot, irec, osend, orec,
     buf_s, src_t, rec_t, buf_b, pgs, rec_y, src_r, rec_r, src_x, rec_x,
     s_in, r_in, s_out, r_out, s_ri, r_ri, s_ro, r_ro,
@@ -196,6 +196,8 @@
             rows = slice(h * BLOCK, (h + 1) * BLOCK)
             qs[g, rows, :] = q_ref[:, cols]
             dos[g, rows, :] = jnp.where(live_rows, do_ref[:, cols].astype(f32), 0.0).astype(bf16)
+    for g in range(2):
+        do_t[g] = dot_nt(eye(HD), dos[g])
     mx[...] = jnp.full(mx.shape, FLOOR, f32)
     sm[...] = jnp.zeros(sm.shape, f32)
     o_t[...] = jnp.zeros(o_t.shape, f32)
@@ -297,29 +299,19 @@
     @pl.loop(0, 2)
     def _(g):
         inv = 1.0 / sm[g]
-        mixed = o_t[g] * inv
-        dl[g] = jnp.sum(dot_nt(eye(HD), dos[g]) * mixed, axis=0, keepdims=True)
+        dl[g] = jnp.sum(do_t[g] * o_t[g], axis=0, keepdims=True) * inv
         sm[g] = inv
-        lane = lax.broadcasted_iota(jnp.int32, (1, ROWS), 1)
-        live = seq * BLOCK + lax.rem(lane, BLOCK) < length
-        rounded = jnp.where(live, mixed, 0.0).astype(bf16)
-        for h in range(GROUP):
-            head = dot_nt(eye(BLOCK), rounded[:, h * BLOCK : (h + 1) * BLOCK])
-            out_ref[:, span(g * GROUP + h, HD)] = head.astype(bf16)
-
-    out_done = pltpu.make_async_copy(out_ref, out_hbm, s_io.at[3])
-    out_done.start()
 
     def bwd(g, c, k, v, p):
-        n = k.shape[0]
         k_t = dot_nt(eye(HD), k).astype(bf16)
         factor = jnp.exp2(mc[g, c] - mx[g]) * sm[g]
         dp = dot_nt(v, dos[g])
         w = p.astype(f32) * factor
         ds = (w * (dp - dl[g])).astype(bf16)
-        acc[1, :n] = dot_nn(w.astype(bf16), dos[g])
-        acc[0, :n] = dot_nn(ds, qs[g]) * SCALE
+        v_grad = dot_nn(w.astype(bf16), dos[g])
+        k_grad = dot_nn(ds, qs[g]) * SCALE
         dq_t[g] += dot_nn(k_t, ds)
+        return k_grad, v_grad
 
     def ri_copy(g, e, k):
         d = steps[k]
@@ -415,18 +407,14 @@
 
         @pl.when(kind == 0)
         def _():
-            bwd(g, 4, buf_b[g * 2], buf_b[g * 2 + 1], pp[g])
-            pgs[g * 2] = acc[0, :PROMPT].astype(bf16)
-            pgs[g * 2 + 1] = acc[1, :PROMPT].astype(bf16)
+            for kv, grad in enumerate(bwd(g, 4, buf_b[g * 2], buf_b[g * 2 + 1], pp[g])):
+                pgs[g * 2 + kv] = grad.astype(bf16)
 
         @pl.when((kind != 0) & jnp.logical_not(none_seen))
         def _():
-            bwd(g, e, kvb[g, e, 0], kvb[g, e, 1], pb[g, e])
-            part[g, e] = acc[...].astype(bf16)
-
-        @pl.when(kind == 4)
-        def _():
-            tot[g] = acc[:, :BLOCK, :]
+            for kv, grad in enumerate(bwd(g, e, kvb[g, e, 0], kvb[g, e, 1], pb[g, e])):
+                part[g, e, kv] = grad.astype(bf16)
+                tot[g, kv] = grad[:BLOCK]
 
         for h in range(2):
             for k, ahead in enumerate((None, 2, 1, 3, 0)):
@@ -444,13 +432,21 @@
     ro_start(1, 1)
     ro_start(0, 3)
 
+    def store_heads(ref, g, transposed):
+        rounded = transposed.astype(bf16)
+        for h in range(GROUP):
+            head = dot_nt(eye(BLOCK), rounded[:, h * BLOCK : (h + 1) * BLOCK])
+            ref[:, span(g * GROUP + h, HD)] = head.astype(bf16)
+
     @pl.loop(0, 2)
     def _(g):
-        rounded = (dq_t[g] * SCALE).astype(bf16)
-        for h in range(GROUP):
-            head = dot_nt(eye(BLOCK), rounded[:, h * BLOCK : (h + 1) * BLOCK])
-            qg_ref[:, span(g * GROUP + h, HD)] = head.astype(bf16)
-
+        lane = lax.broadcasted_iota(jnp.int32, (1, ROWS), 1)
+        live = seq * BLOCK + lax.rem(lane, BLOCK) < length
+        store_heads(out_ref, g, jnp.where(live, o_t[g] * sm[g], 0.0))
+        store_heads(qg_ref, g, dq_t[g] * SCALE)
+
+    out_done = pltpu.make_async_copy(out_ref, out_hbm, s_io.at[3])
+    out_done.start()
     ro_start(1, 3)
     qg_done = pltpu.make_async_copy(qg_ref, qg_hbm, s_io.at[4])
     qg_done.start()
@@ -543,7 +539,7 @@
             pltpu.VMEM((2, HD, ROWS), f32),
             pltpu.VMEM((2, HD, ROWS), f32),
             pltpu.VMEM((2, 1, ROWS), f32),
-            pltpu.VMEM((2, SLAB, HD), f32),
+            pltpu.VMEM((2, HD, ROWS), f32),
             pltpu.VMEM((2, 4, 2, SLAB, HD), bf16),
             pltpu.VMEM((2, 2, BLOCK, HD), f32),
             pltpu.VMEM((2, 2, BLOCK, HD), f32),

time: 60.8 us -> 60.2 us (level)
  no operation moved by 1% of the time
where the time goes in v4:
time: 60.2 us; the launch traced here: 60.1 us
  Pallas kernels  58.8 us (98%)
  between operations  1.29 us (2%)
    pallas_call x1, Pallas kernels, shards(): pl.pallas_call(kernel, out_shape=out_shape, in_specs=[pl.BlockSpec(memory...  56.4 us
    pallas_call x1, Pallas kernels, shards(): pl.pallas_call(store_kernel, out_shape=out_shape, in_specs=[vmem] * 4, ou...  2.35 us

profile of v4, /device:TPU:4, one launch (start us, length us, event | category | flops | bytes accessed | tf_op | source)
XLA Modules:
  0.0 60.1 jit_solution(15593000426184152102)
XLA Ops:
  1.3 56.4 %shard_map.84 = (bf16[128,2048]{1,0:T(8,128)(2,1)}, bf16[128,2048]{1,0:T(8,128)(2,1)}, f32[2,128,256]{2,1,0:T(8,128)}, f32[2,4,256]{2,1,0:T(4,128)}) custom-call(s32[1]{0:T(128)S(6)} %copy.10.len_ref, bf16[2,1024]{1,0:T(2,128)(2,1)} %bitcast.12, bf16[128,2048]{1,0:T(8,128)(2,1)} %bitcast.9, bf16[2,128,256]{2,1,0:T(8,128)(2,1)} %bitcast.11, ...), custom_call_target="tpu_custom_call" | custom-call | tf_op jit(solution)/shard_map/pallas_call | solution.py:518
  57.7 2.4 %shard_map.85 = (bf16[128,2048]{1,0:T(8,128)(2,1)}, bf16[128,2048]{1,0:T(8,128)(2,1)}, f32[2,128,256]{2,1,0:T(8,128)}, f32[2,4,256]{2,1,0:T(4,128)}) custom-call(bf16[128,2048]{1,0:T(8,128)(2,1)} %get-tuple-element.12.a, bf16[128,2048]{1,0:T(8,128)(2,1)} %get-tuple-element.13.b, f32[2,128,256]{2,1,0:T(8,128)} %get-tuple-element.14.c, ...), custom_call_target="tpu_custom_call" | custom-call | tf_op jit(solution)/shard_map/pallas_call | solution.py:569

commit v5 on v4

--- a/solution.py
+++ b/solution.py
@@ -112,6 +112,10 @@
         def _():
             kvb[0, 0, :, p * BLOCK : (p + 1) * BLOCK, :] = jnp.zeros((2, BLOCK, HD), bf16)
 
+        @pl.when((y == 3) & (x + p < 4))
+        def _():
+            kvb[1, p, :, :BLOCK, :] = jnp.zeros((2, BLOCK, HD), bf16)
+
     pl.semaphore_wait(barrier, 12)
 
     def seen_slab(g, e, act):
@@ -125,11 +129,22 @@
         src = kvb.at[g, 0, :, :BLOCK, :]
         return rcopy(src, kvb.at[g, 4 - d, :, :BLOCK, :], s_out.at[g, k], r_out.at[g, k], outer(g, d))
 
+    def outer_sent(g, k, act):
+        d = steps[k]
+        pl.when(y + d < 4 if g == 0 else (y < 3) | (x + d < 4))(act)
+
+    def outer_seen(g, k, act):
+        d = steps[k]
+        pl.when(y >= d if g == 0 else (y < 3) | (x >= d))(act)
+
+    def sum_sent(g, e, act):
+        pl.when(y + e >= 4 if g == 0 else (y < 3) | (x + e >= 4))(act)
+
+    def sum_seen(g, e, act):
+        pl.when(y < e if g == 0 else (y < 3) | (x < e))(act)
+
     def outer_start(g, k):
-        def act():
-            outer_copy(g, k).start()
-
-        pl.when(y + steps[k] < 4)(act) if g == 0 else act()
+        outer_sent(g, k, lambda: outer_copy(g, k).start())
 
     def inner_copy(g, e, k):
         d = steps[k]
@@ -180,10 +195,10 @@
         for k in range(3):
             prompt_copies[stage](k, 4 - steps[k]).wait_recv()
 
+    prompt_start(0)
     for k in range(3):
         for g in range(2):
             outer_start(g, k)
-    prompt_start(0)
     for g in range(2):
         inner_start(g, 0)
 
@@ -213,7 +228,7 @@
     def pass_on(k):
         for g in range(2):
             e = 4 - steps[k]
-            seen_slab(g, e, lambda: outer_copy(g, k).wait_recv())
+            outer_seen(g, k, lambda: outer_copy(g, k).wait_recv())
             inner_start(g, e)
 
     pass_on(0)
@@ -347,7 +362,7 @@
             osend[g, e] = own[g].astype(bf16)
             ro_copy(g, e).start()
 
-        seen_slab(g, e, act)
+        sum_sent(g, e, act)
 
     def cy_copy(k, from_offset):
         src = pgs.at[:, span(rem4(y + steps[k]), 64), :]
@@ -464,7 +479,7 @@
                 ro_copy(g, e).wait_recv()
                 tot[g] += orec[g, e].astype(f32)
 
-            pl.when(y < e)(add_outer) if g == 0 else add_outer()
+            sum_seen(g, e, add_outer)
         for kv in range(2):
             okv_ref[kv, :, g * HD : (g + 1) * HD] = tot[g, kv]
     okv_done = pltpu.make_async_copy(okv_ref, okv_hbm, s_io.at[5])
@@ -483,9 +498,9 @@
             inner_do(g, e, True, lambda k: inner_copy(g, e, k).wait_send())
             ri_do(g, e, True, lambda k: ri_copy(g, e, k).wait_send())
             if e > 0:
-                seen_slab(g, e, lambda: ro_copy(g, e).wait_send())
+                sum_sent(g, e, lambda: ro_copy(g, e).wait_send())
         for k in range(3):
-            pl.when(y + steps[k] < 4)(lambda: outer_copy(g, k).wait_send()) if g == 0 else outer_copy(g, k).wait_send()
+            outer_sent(g, k, lambda: outer_copy(g, k).wait_send())
     for k in range(3):
         for copy in prompt_copies + sum_copies:
             copy(k, 0).wait_send()

time: 60.2 us -> 59.3 us (0.985)
  Pallas kernels: 58.8 us -> 57.8 us
    pallas_call x1, Pallas kernels: 56.4 us -> 55.4 us  [shards(): pl.pallas_call(kernel, out_shape=out_shape, in_specs=[pl.BlockSpec(memory...]
where the time goes in v5:
time: 59.3 us; the launch traced here: 59 us
  Pallas kernels  57.8 us (97%)
  between operations  1.29 us (2%)
    pallas_call x1, Pallas kernels, shards(): pl.pallas_call(kernel, out_shape=out_shape, in_specs=[pl.BlockSpec(memory...  55.4 us
    pallas_call x1, Pallas kernels, shards(): pl.pallas_call(store_kernel, out_shape=out_shape, in_specs=[vmem] * 4, ou...  2.35 us

profile of v5, /device:TPU:4, one launch (start us, length us, event | category | flops | bytes accessed | tf_op | source)
XLA Modules:
  0.0 59.0 jit_solution(11184606458593951599)
XLA Ops:
  1.3 55.4 %shard_map.84 = (bf16[128,2048]{1,0:T(8,128)(2,1)}, bf16[128,2048]{1,0:T(8,128)(2,1)}, f32[2,128,256]{2,1,0:T(8,128)}, f32[2,4,256]{2,1,0:T(4,128)}) custom-call(s32[1]{0:T(128)S(6)} %copy.10.len_ref, bf16[2,1024]{1,0:T(2,128)(2,1)} %bitcast.12, bf16[128,2048]{1,0:T(8,128)(2,1)} %bitcast.9, bf16[2,128,256]{2,1,0:T(8,128)(2,1)} %bitcast.11, ...), custom_call_target="tpu_custom_call" | custom-call | tf_op jit(solution)/shard_map/pallas_call | solution.py:533
  56.7 2.4 %shard_map.85 = (bf16[128,2048]{1,0:T(8,128)(2,1)}, bf16[128,2048]{1,0:T(8,128)(2,1)}, f32[2,128,256]{2,1,0:T(8,128)}, f32[2,4,256]{2,1,0:T(4,128)}) custom-call(bf16[128,2048]{1,0:T(8,128)(2,1)} %get-tuple-element.12.a, bf16[128,2048]{1,0:T(8,128)(2,1)} %get-tuple-element.13.b, f32[2,128,256]{2,1,0:T(8,128)} %get-tuple-element.14.c, ...), custom_call_target="tpu_custom_call" | custom-call | tf_op jit(solution)/shard_map/pallas_call | solution.py:584

commit v6 on v5

--- a/solution.py
+++ b/solution.py
@@ -294,7 +294,7 @@
                 buf_b[j, span(y * 4 + roll, 16), :] = jnp.concatenate(rows, axis=0).astype(bf16)
             prompt_start(2)
 
-        @pl.when(i == 4)
+        @pl.when(i == 3)
         def _():
             prompt_wait(2)
             prompt_start(3)

time: 59.3 us -> 59.5 us (level); the launches traced: 59 us -> 58.5 us
  Pallas kernels: 57.8 us -> 57.2 us
where the time goes in v6:
time: 59.5 us; the launch traced here: 58.5 us
  Pallas kernels  57.2 us (96%)
  between operations  1.29 us (2%)
    pallas_call x1, Pallas kernels, shards(): pl.pallas_call(kernel, out_shape=out_shape, in_specs=[pl.BlockSpec(memory...  54.9 us
    pallas_call x1, Pallas kernels, shards(): pl.pallas_call(store_kernel, out_shape=out_shape, in_specs=[vmem] * 4, ou...  2.35 us

profile of v6, /device:TPU:4, one launch (start us, length us, event | category | flops | bytes accessed | tf_op | source)
XLA Modules:
  0.0 58.5 jit_solution(5251851312911482524)
XLA Ops:
  1.3 54.9 %shard_map.84 = (bf16[128,2048]{1,0:T(8,128)(2,1)}, bf16[128,2048]{1,0:T(8,128)(2,1)}, f32[2,128,256]{2,1,0:T(8,128)}, f32[2,4,256]{2,1,0:T(4,128)}) custom-call(s32[1]{0:T(128)S(6)} %copy.10.len_ref, bf16[2,1024]{1,0:T(2,128)(2,1)} %bitcast.12, bf16[128,2048]{1,0:T(8,128)(2,1)} %bitcast.9, bf16[2,128,256]{2,1,0:T(8,128)(2,1)} %bitcast.11, ...), custom_call_target="tpu_custom_call" | custom-call | tf_op jit(solution)/shard_map/pallas_call | solution.py:533
  56.1 2.4 %shard_map.85 = (bf16[128,2048]{1,0:T(8,128)(2,1)}, bf16[128,2048]{1,0:T(8,128)(2,1)}, f32[2,128,256]{2,1,0:T(8,128)}, f32[2,4,256]{2,1,0:T(4,128)}) custom-call(bf16[128,2048]{1,0:T(8,128)(2,1)} %get-tuple-element.12.a, bf16[128,2048]{1,0:T(8,128)(2,1)} %get-tuple-element.13.b, f32[2,128,256]{2,1,0:T(8,128)} %get-tuple-element.14.c, ...), custom_call_target="tpu_custom_call" | custom-call | tf_op jit(solution)/shard_map/pallas_call | solution.py:584
